TPU v7x, 256 devices: a whole 4x4x8 slice. The times are simulated.
256 devices in a mesh: dp: 64 (over z_lo, y, x, core), grp: 4 (over z_hi).
Axes of the slice: x: 4, y: 4, z: 8 (z_hi: 4, z_lo: 2; z = z_hi * 2 + z_lo), core: 2. Of those that a mesh axis runs over, the one named last changes fastest.
Arguments:
- patches: bfloat16 [1, 524288, 1152], P(None, ('dp', 'grp')), may hold values from -24 to 24
- out_grads: bfloat16 [1, 524288, 128], P(None, ('dp', 'grp')), may hold values from -6 to 6
- counts: int32 [256], P(('dp', 'grp')), may hold values from 682 to 2048, as said below
- basis_a: bfloat16 [1, 1152, 1152], replicated, may hold values from -0.1875 to 0.1875
- basis_g: bfloat16 [1, 128, 128], replicated, may hold values from -0.5 to 0.5
- eig_a: float32 [1, 1152], replicated, may hold values from 0.5 to 5
- eig_g: float32 [1, 128], replicated, may hold values from 0.001 to 0.01
Outputs:
- a_factor: float32 [1, 1152, 1152], P(None, 'dp')
- g_factor: float32 [1, 128, 128], replicated
- precond: float32 [1, 128, 1152], replicated
Inputs may be any that keep to these rules, and one draw needn't show every extreme that they name: counts rise roughly evenly with the device index from about 2048 // 3 to 2048; the last device has exactly 2048.
All inputs are finite; a program needn't handle non-finite values.
Results may differ from a plain program's by a relative error of at most 0.0065.
Values sent between devices are 32-bit elements; how exact they have to be, the bound alone decides.
No kernel may reach another device: no remote copies, remote signals or barrier semaphores. Data moves between devices by JAX's collectives and lax.ppermute only.
A program may use at most 64 MiB of HBM per device.

v0:
```python
import jax
import jax.numpy as jnp
from jax import lax
from jax.experimental import pallas as pl
from jax.experimental.pallas import tpu as pltpu
from jax.sharding import Mesh, PartitionSpec as P

DA, DG, ROWS = 1152, 128, 2048
WIDTH = DA + DG
PARTS = (0, 512, ROWS)
BLOCKS = DA // 128
HALF = BLOCKS // 2 + 1
CHIPS, SLOTS, GRADS = 32, 14, 3
LOW = SLOTS - GRADS
CHIP_AXES = ("zl", "y", "xh", "xl")
HBM = pltpu.MemorySpace.HBM
F32, BF16 = jnp.float32, jnp.bfloat16


def factor_slot(v):
    return (0, GRADS + v) if v < LOW else (1, GRADS - 1 + v - LOW)


def factor_places(row8, step):
    group, within = divmod(row8, 9)
    if within == 4:
        core, slot = factor_slot(4 * HALF + step // 2)
        to = slice(4 * (step % 2), 4 * (step % 2) + 4)
        for xl in (0, 1):
            yield (core, 2 * group + xl, slot, to), slice(4 * xl, 4 * xl + 4)
    else:
        xl = within // 5
        core, slot = factor_slot((within - 5 * xl) * HALF + step)
        yield (core, 2 * group + xl, slot, slice(0, 8)), slice(0, 8)


def grad_place(row8, col):
    chip, rest = divmod(row8 * 10 + col, 5)
    return (0, chip, rest, slice(0, 8)) if rest < 3 else (1, chip, rest - 3, slice(0, 8))


def position():
    group = (lax.axis_index("zl") * 4 + lax.axis_index("y")) * 2 + lax.axis_index("xh")
    return group, lax.axis_index("xl"), lax.axis_index("core")


def products(part, z, zt, acc):
    depth = slice(PARTS[part], PARTS[part + 1])

    def put(place, tile):
        acc[place] = acc[place] + tile if part else tile

    for col0 in range(0, BLOCKS + 1, 2):
        wanted = sorted({(c - s) % BLOCKS for c in (col0, col0 + 1) if c < BLOCKS for s in range(HALF)}) + [BLOCKS]
        runs = []
        for i in wanted:
            if runs and runs[-1][-1] == i - 1:
                runs[-1].append(i)
            else:
                runs.append([i])
        for run in runs:
            w = jnp.dot(
                zt[128 * run[0] : 128 * run[-1] + 128, depth],
                z[depth, 128 * col0 : 128 * col0 + 256],
                preferred_element_type=F32,
            )
            for u in range(16 * len(run)):
                row8 = 16 * run[0] + u
                for v in (0, 1):
                    tile = w[8 * u : 8 * u + 8, 128 * v : 128 * v + 128]
                    if row8 >= DA // 8:
                        put(grad_place(row8 - DA // 8, col0 + v), tile)
                    elif col0 + v < BLOCKS and (col0 + v - row8 // 16) % BLOCKS < HALF:
                        for place, rows in factor_places(row8, (col0 + v - row8 // 16) % BLOCKS):
                            put(place, tile[rows])


def gram_kernel(count_ref, x_hbm, y_hbm, mine, theirs, z, zt, acc, in_sem, out_sem):
    copies = []
    for k in range(len(PARTS) - 1):
        rows = pl.ds(PARTS[k], PARTS[k + 1] - PARTS[k])
        copies.append(
            (
                pltpu.make_async_copy(x_hbm.at[0, rows, :], z.at[rows, pl.ds(0, DA)], in_sem.at[k, 0]),
                pltpu.make_async_copy(y_hbm.at[0, rows, :], z.at[rows, pl.ds(DA, DG)], in_sem.at[k, 1]),
            )
        )
        for copy in copies[k]:
            copy.start()
    count, core = count_ref[0], lax.axis_index("core")
    acc[1, :, SLOTS - 1, 4:8, :] = jnp.full((CHIPS, 4, 128), count.astype(F32))
    for k in range(len(PARTS) - 1):
        for copy in copies[k]:
            copy.wait()
        here = slice(PARTS[k], PARTS[k + 1])
        row = lax.broadcasted_iota(jnp.int32, (PARTS[k + 1] - PARTS[k], 1), 0) + PARTS[k]
        zt[:, here] = jnp.where(row < count, z[here, :], jnp.zeros((), BF16)).T
        products(k, z, zt, acc)
    first = pltpu.make_async_copy(acc.at[1 - core], theirs, out_sem.at[0])
    second = pltpu.make_async_copy(acc.at[core], mine, out_sem.at[1])
    first.start()
    second.start()
    first.wait()
    second.wait()


def gram(patches, out_grads, counts):
    half = jax.ShapeDtypeStruct((CHIPS, SLOTS, 8, 128), F32)
    return pl.pallas_call(
        gram_kernel,
        out_shape=(half, half),
        in_specs=[pl.BlockSpec(memory_space=pltpu.SMEM)] + [pl.BlockSpec(memory_space=HBM)] * 2,
        out_specs=(pl.BlockSpec(memory_space=HBM),) * 2,
        scratch_shapes=[
            pltpu.VMEM((ROWS, WIDTH), BF16),
            pltpu.VMEM((WIDTH, ROWS), BF16),
            pltpu.VMEM((2, CHIPS, SLOTS, 8, 128), F32),
            pltpu.SemaphoreType.DMA((len(PARTS) - 1, 2)),
            pltpu.SemaphoreType.DMA((2,)),
        ],
        compiler_params=pltpu.CompilerParams(vmem_limit_bytes=48 * 2**20),
        cost_estimate=pl.CostEstimate(flops=2 * ROWS * WIDTH * WIDTH, bytes_accessed=10 * 2**20, transcendentals=0),
        name="gram",
    )(counts, patches, out_grads)


def collect_kernel(met, out):
    total = met[0]
    for n in range(1, CHIPS):
        total = total + met[n]
    out[...] = total


def collect(met):
    return pl.pallas_call(
        collect_kernel,
        out_shape=jax.ShapeDtypeStruct((SLOTS, 8, 128), F32),
        compiler_params=pltpu.CompilerParams(vmem_limit_bytes=16 * 2**20),
        name="collect",
    )(met)


def spread_kernel(done, twin, send, direct, total, flat):
    group, xl, core = position()
    own, other = done[...], twin[...]
    low = jnp.where(core == 0, own, other)
    high = jnp.where(core == 0, other, own)
    total[...] = jnp.broadcast_to(high[SLOTS - 1, 4:5], (8, 128))
    direct[...] = jnp.zeros_like(direct)
    shared = (9 * group + 4) // 16
    for v in range(4 * HALF + HALF // 2 + 1):
        here, slot = factor_slot(v)
        tile = high[slot] if here else low[slot]
        u, step = divmod(v, HALF)
        if u < 4:
            col = lax.rem((9 * group + 5 * xl + u) // 16 + step, BLOCKS)
            direct[col, 8 * u : 8 * u + 8, :] = tile
        else:
            direct[lax.rem(shared + 2 * step, BLOCKS), 32:36, :] = tile[0:4]
            if 2 * step + 1 < HALF:
                direct[lax.rem(shared + 2 * step + 1, BLOCKS), 32:36, :] = tile[4:8]
    pad = jnp.zeros((128 - 40, 128), F32)
    for col in range(BLOCKS):
        flat[0, 128 * col : 128 * col + 128, :] = jnp.concatenate([direct[col], pad], axis=0).T
    flat[0, DA : DA + 8, :] = jnp.zeros((8, 128), F32)
    for third in (1, 2):
        flat[third] = pltpu.roll(flat[0], 40 * third, 1)
    send[:, :GRADS] = jnp.broadcast_to(own[None, :GRADS], (CHIPS, GRADS, 8, 128))
    for here in (0, 1):

        @pl.when(core == here)
        def _():
            for n in range(CHIPS):
                first = 36 * n + 18 * here
                thirds = [flat[t, first + 6 * t : first + 6 * t + 8, :] for t in range(3)]
                send[n, GRADS] = thirds[0] + thirds[1] + thirds[2]


def spread(done, twin):
    vmem = pl.BlockSpec(memory_space=pltpu.VMEM)
    return pl.pallas_call(
        spread_kernel,
        out_shape=(
            jax.ShapeDtypeStruct((CHIPS, GRADS + 1, 8, 128), F32),
            jax.ShapeDtypeStruct((BLOCKS, 40, 128), F32),
            jax.ShapeDtypeStruct((8, 128), F32),
        ),
        in_specs=[vmem, vmem],
        out_specs=(vmem,) * 3,
        scratch_shapes=[pltpu.VMEM((3, DA + 8, 128), F32)],
        compiler_params=pltpu.CompilerParams(vmem_limit_bytes=16 * 2**20),
        name="spread",
    )(done, twin)


def rows_kernel(got, direct, total_ref, out, turned):
    group, xl, core = position()
    total = total_ref[0:1, 0:1]
    for n in range(CHIPS):
        for third in range(3):
            rows = slice(6 * third, 6 * third + 6)
            for to, first, size in ((4, 0, 32), (0, 32, 4)) if n % 2 else ((0, 0, 36),):
                first = first + 40 * third
                turned[rows, 36 * n + to : 36 * n + to + size] = got[n, GRADS, 0:6, first : first + size]
    start = 72 * group + 36 * xl + 18 * core
    block = (lax.broadcasted_iota(jnp.int32, (18, 128), 0) + start) // 128
    for here in range(4):

        @pl.when(2 * xl + core == here)
        def _():
            first = (0, 18, 0, 14)[here]
            for col in range(BLOCKS):
                step = col - block
                step = jnp.where(step < 0, step + BLOCKS, step)
                lanes = slice(128 * col, 128 * col + 128)
                if here == 2:
                    straight = jnp.concatenate([direct[col, 32:36, :], direct[col, 0:14, :]], axis=0)
                else:
                    straight = direct[col, first : first + 18, :]
                value = jnp.where(step < HALF, straight, turned[:18, lanes]) / total
                for i in range(18):
                    out[i, :, lanes] = value[i : i + 1, :]


def factor_rows(got, direct, total):
    vmem = pl.BlockSpec(memory_space=pltpu.VMEM)
    out = pl.pallas_call(
        rows_kernel,
        out_shape=jax.ShapeDtypeStruct((18, 1, DA), F32),
        in_specs=[vmem] * 3,
        scratch_shapes=[pltpu.VMEM((24, DA), F32)],
        compiler_params=pltpu.CompilerParams(vmem_limit_bytes=16 * 2**20),
        cost_estimate=pl.CostEstimate(flops=10**6, bytes_accessed=2**20, transcendentals=0),
        name="factor_rows",
    )(got, direct, total)
    return out.reshape(1, 18, DA)


def precond_kernel(got, other, total_ref, basis_a, basis_g, eig_a, eig_g, g_factor, precond):
    core = lax.axis_index("core")
    total = total_ref[0:1, 0:1]
    shape = (16, 2, GRADS + 1, 8, 128)
    both = (got[...].reshape(shape), other[...].reshape(shape))
    columns = []
    for col in range(WIDTH // 128):
        n, rest = divmod(col, 5)
        low, rest = (rest < 3), (rest if rest < 3 else rest - 3)
        tiles = jnp.where((core == 0) == low, both[0][:, n, rest], both[1][:, n, rest])
        columns.append(tiles.reshape(128, 128) / total)
    g_factor[0] = columns[-1]
    grad = jnp.concatenate([c.astype(BF16) for c in columns[:-1]], axis=1)
    left = lax.dot_general(basis_g[0], grad, (((0,), (0,)), ((), ())), preferred_element_type=F32).astype(BF16)
    rotated = jnp.dot(left, basis_a[0], preferred_element_type=F32)
    eig_rows = jnp.broadcast_to(eig_g[...], (DG, DG)).T[:, 0:1]
    scaled = (rotated / (eig_rows * eig_a[...] + 0.001)).astype(BF16)
    inner = jnp.dot(basis_g[0], scaled, preferred_element_type=F32).astype(BF16)
    precond[0] = lax.dot_general(inner, basis_a[0], (((1,), (1,)), ((), ())), preferred_element_type=F32)


def precondition(got, other, total, basis_a, basis_g, eig_a, eig_g):
    vmem = pl.BlockSpec(memory_space=pltpu.VMEM)
    return pl.pallas_call(
        precond_kernel,
        out_shape=(jax.ShapeDtypeStruct((1, DG, DG), F32), jax.ShapeDtypeStruct((1, DG, DA), F32)),
        in_specs=[vmem] * 7,
        compiler_params=pltpu.CompilerParams(vmem_limit_bytes=16 * 2**20),
        name="precondition",
    )(got, other, total, basis_a, basis_g, eig_a, eig_g)


def swap_cores(value):
    return lax.ppermute(value, "core", [(0, 1), (1, 0)])


def group_sums(value):
    value = value + lax.ppermute(value, "zh", [(i, i ^ 1) for i in range(4)])
    far = lax.ppermute(value, "zh", [(i, i ^ 3) for i in range(4)])
    twin = swap_cores(value)
    twin_far = lax.ppermute(value, ("core", "zh"), [(i, i ^ 7) for i in range(8)])
    return value + far, twin + twin_far


def on_device(patches, out_grads, counts, basis_a, basis_g, eig_a, eig_g):
    mine, theirs = gram(patches, out_grads, counts)
    met = lax.all_to_all(mine + swap_cores(theirs), CHIP_AXES, 0, 0, tiled=True)
    send, direct, total = spread(*group_sums(collect(met)))
    got = lax.all_to_all(send, CHIP_AXES, 0, 0, tiled=True)
    other = swap_cores(got)
    a_factor = factor_rows(got, direct, total)
    g_factor, precond = precondition(got, other, total, basis_a, basis_g, eig_a, eig_g)
    return a_factor, g_factor, precond


def solution(mesh):
    axes = ("zl", "y", "xh", "xl", "core", "zh")
    finer = Mesh(mesh.devices.reshape(2, 4, 2, 2, 2, 4), axes)
    placed = (P(None, axes, None), P(None, axes, None), P(axes), P(), P(), P(), P())
    return jax.shard_map(
        on_device,
        mesh=finer,
        in_specs=placed,
        out_specs=(P(None, axes[:-1], None), P(), P()),
        check_vma=False,
    )
```

profile of v0, /device:TPU:1, one launch (start us, length us, event | category | flops | bytes accessed | tf_op | source)
XLA Modules:
  0.0 86.1 jit_solution(1949834100114709447)
XLA Ops:
  1.3 0.0 copy-start.4
  1.3 1.0 %copy-done.4 = bf16[1,2048,128]{2,1,0:T(8,128)(2,1)S(1)} copy-done((bf16[1,2048,128]{2,1,0:T(8,128)(2,1)S(1)}, bf16[1,2048,128]{2,1,0:T(8,128)(2,1)}, u32[]{:S(2)}) %copy-start.4) | copy-done | bytes 524312
  2.3 7.4 %gram.1 = (f32[32,14,8,128]{3,2,1,0:T(8,128)S(1)}, f32[32,14,8,128]{3,2,1,0:T(8,128)S(1)}) custom-call(s32[1]{0:T(128)S(6)} %copy.10.count_ref, bf16[1,2048,1152]{2,1,0:T(8,128)(2,1)} %x_hbm.1, bf16[1,2048,128]{2,1,0:T(8,128)(2,1)S(1)} %copy-done.4), custom_call_target="tpu_custom_call" | custom-call | flops 6710886400 | bytes 10485760 | tf_op jit(solution)/shard_map/gram/pallas_call | solution.py:109
  9.8 3.3 %collective-permute-start = (f32[32,14,8,128]{3,2,1,0:T(8,128)S(1)}, f32[32,14,8,128]{3,2,1,0:T(8,128)S(1)}, u32[]{:S(2)}, u32[]{:S(2)}) collective-permute-start(f32[32,14,8,128]{3,2,1,0:T(8,128)S(1)} %get-tuple-element.11), channel_id=1, source_target_pairs={{0,4},{4,0},{1,5},{5,1},{2,6},{6,2},{3,7},{7,3},{8,12},{12,8},{9,1... | collective-permute-start | bytes 5505032 | tf_op jit(solution)/shard_map/ppermute | solution.py:272
  13.1 3.4 %collective-permute-done = f32[32,14,8,128]{3,2,1,0:T(8,128)S(1)} collective-permute-done((f32[32,14,8,128]{3,2,1,0:T(8,128)S(1)}, f32[32,14,8,128]{3,2,1,0:T(8,128)S(1)}, u32[]{:S(2)}, u32[]{:S(2)}) %collective-permute-start) | collective-permute-done | bytes 1835040 | tf_op jit(solution)/shard_map/ppermute | solution.py:272
  16.5 0.3 add.12
  16.9 30.2 %all_to_all.10.met = f32[32,14,8,128]{3,2,1,0:T(8,128)S(1)} all-to-all(f32[32,14,8,128]{3,2,1,0:T(8,128)S(1)} %add.12), channel_id=1, replica_groups=mesh['zl'=2,'y'=4,'xh'=2,'xl'=2,'core'=2,'zh'=4] {'zl','y','xh','xl'}, dimensions={0} | all-to-all | bytes 3670016 | tf_op jit(solution)/shard_map/all_to_all | solution.py:285
  47.1 0.0 copy-start
  47.1 0.0 copy-start.1
  47.1 0.0 copy-start.2
  47.1 0.0 copy-start.3
  47.1 0.1 collect.1
  47.2 3.1 %collective-permute-start.1 = (f32[14,8,128]{2,1,0:T(8,128)S(1)}, f32[14,8,128]{2,1,0:T(8,128)S(1)}, u32[]{:S(2)}, u32[]{:S(2)}) collective-permute-start(f32[14,8,128]{2,1,0:T(8,128)S(1)} %collect.1), channel_id=1, source_target_pairs={{0,1},{1,0},{2,3},{3,2},{4,5},{5,4},{6,7},{7,6},{8,9},{9,8},{10,11... | collective-permute-start | bytes 172040 | tf_op jit(solution)/shard_map/ppermute | solution.py:276
  50.2 1.6 %collective-permute-done.1 = f32[14,8,128]{2,1,0:T(8,128)S(1)} collective-permute-done((f32[14,8,128]{2,1,0:T(8,128)S(1)}, f32[14,8,128]{2,1,0:T(8,128)S(1)}, u32[]{:S(2)}, u32[]{:S(2)}) %collective-permute-start.1) | collective-permute-done | bytes 57376 | tf_op jit(solution)/shard_map/ppermute | solution.py:276
  51.8 4.6 %collective-permute-start.2 = (f32[14,8,128]{2,1,0:T(8,128)S(1)}, f32[14,8,128]{2,1,0:T(8,128)S(1)}, u32[]{:S(2)}, u32[]{:S(2)}) collective-permute-start(f32[14,8,128]{2,1,0:T(8,128)S(1)} %add.13), channel_id=1, source_target_pairs={{0,3},{1,2},{2,1},{3,0},{4,7},{5,6},{6,5},{7,4},{8,11},{9,10},{10,... | collective-permute-start | bytes 172040 | tf_op jit(solution)/shard_map/ppermute | solution.py:277
  56.4 3.7 %collective-permute-start.4 = (f32[14,8,128]{2,1,0:T(8,128)S(1)}, f32[14,8,128]{2,1,0:T(8,128)S(1)}, u32[]{:S(2)}, u32[]{:S(2)}) collective-permute-start(f32[14,8,128]{2,1,0:T(8,128)S(1)} %add.13), channel_id=1, source_target_pairs={{0,7},{1,6},{2,5},{3,4},{4,3},{5,2},{6,1},{7,0},{8,15},{9,14},{10,... | collective-permute-start | bytes 172040 | tf_op jit(solution)/shard_map/ppermute | solution.py:279
  60.1 0.3 collective-permute-start.3
  60.4 0.0 collective-permute-done.2
  60.4 2.2 %collective-permute-done.4 = f32[14,8,128]{2,1,0:T(8,128)S(1)} collective-permute-done((f32[14,8,128]{2,1,0:T(8,128)S(1)}, f32[14,8,128]{2,1,0:T(8,128)S(1)}, u32[]{:S(2)}, u32[]{:S(2)}) %collective-permute-start.4) | collective-permute-done | bytes 57376 | tf_op jit(solution)/shard_map/ppermute | solution.py:279
  62.6 0.0 collective-permute-done.3
  62.6 0.7 spread.1
  63.3 14.4 %all_to_all.11.got = f32[32,4,8,128]{3,2,1,0:T(8,128)S(1)} all-to-all(f32[32,4,8,128]{3,2,1,0:T(8,128)S(1)} %get-tuple-element.12), channel_id=1, replica_groups=mesh['zl'=2,'y'=4,'xh'=2,'xl'=2,'core'=2,'zh'=4] {'zl','y','xh','xl'}, dimensions={0} | all-to-all | bytes 1048576 | tf_op jit(solution)/shard_map/all_to_all | solution.py:287
  77.7 4.4 %collective-permute-start.5 = (f32[32,4,8,128]{3,2,1,0:T(8,128)S(1)}, f32[32,4,8,128]{3,2,1,0:T(8,128)S(1)}, u32[]{:S(2)}, u32[]{:S(2)}) collective-permute-start(f32[32,4,8,128]{3,2,1,0:T(8,128)S(1)} %all_to_all.11.got), channel_id=1, source_target_pairs={{0,4},{4,0},{1,5},{5,1},{2,6},{6,2},{3,7},{7,3},{8,12},{12,8},{9,1... | collective-permute-start | bytes 1572872 | tf_op jit(solution)/shard_map/ppermute | solution.py:272
  82.1 0.9 %factor_rows.1 = f32[18,1,1152]{2,1,0:T(1,128)} custom-call(f32[32,4,8,128]{3,2,1,0:T(8,128)S(1)} %all_to_all.11.got, f32[9,40,128]{2,1,0:T(8,128)S(1)} %get-tuple-element.13.direct, f32[8,128]{1,0:T(8,128)S(1)} %get-tuple-element.14.total_ref), custom_call_target="tpu_custom_call" | custom-call | flops 1000000 | bytes 1048576 | tf_op jit(solution)/shard_map/factor_rows/pallas_call | solution.py:227
  83.0 0.6 collective-permute-done.5.other
  83.6 0.0 copy-done
  83.6 0.0 copy-done.1
  83.6 0.0 copy-done.2
  83.6 0.0 copy-done.3
  83.6 2.5 %precondition.1 = (f32[1,128,128]{2,1,0:T(8,128)}, f32[1,128,1152]{2,1,0:T(8,128)}) custom-call(f32[32,4,8,128]{3,2,1,0:T(8,128)S(1)} %all_to_all.11.got, f32[32,4,8,128]{3,2,1,0:T(8,128)S(1)} %collective-permute-done.5.other, f32[8,128]{1,0:T(8,128)S(1)} %get-tuple-element.14.total_ref, bf16[1,1152,1152]{2,1,0:T(8,128)(2,1)S(1)} %copy-done, ...), custom_call_target="tpu_custom_call" | custom-call | tf_op jit(solution)/shard_map/precondition/pallas_call | solution.py:262
  (3 shorter events, 0.0 us)
Async XLA Ops:
  1.3 1.0 %copy-start.4 = (bf16[1,2048,128]{2,1,0:T(8,128)(2,1)S(1)}, bf16[1,2048,128]{2,1,0:T(8,128)(2,1)}, u32[]{:S(2)}) copy-start(bf16[1,2048,128]{2,1,0:T(8,128)(2,1)} %y_hbm.1) | copy-start | bytes 1572868
  9.8 6.7 %collective-permute-start = (f32[32,14,8,128]{3,2,1,0:T(8,128)S(1)}, f32[32,14,8,128]{3,2,1,0:T(8,128)S(1)}, u32[]{:S(2)}, u32[]{:S(2)}) collective-permute-start(f32[32,14,8,128]{3,2,1,0:T(8,128)S(1)} %get-tuple-element.11), channel_id=1, source_target_pairs={{0,4},{4,0},{1,5},{5,1},{2,6},{6,2},{3,7},{7,3},{8,12},{12,8},{9,1... | collective-permute-start | bytes 5505032 | tf_op jit(solution)/shard_map/ppermute | solution.py:272
  47.1 36.6 %copy-start = (bf16[1,1152,1152]{2,1,0:T(8,128)(2,1)S(1)}, bf16[1,1152,1152]{2,1,0:T(8,128)(2,1)}, u32[]{:S(2)}) copy-start(bf16[1,1152,1152]{2,1,0:T(8,128)(2,1)} %basis_a.1) | copy-start | bytes 7962628
  47.1 36.6 %copy-start.1 = (bf16[1,128,128]{2,1,0:T(8,128)(2,1)S(1)}, bf16[1,128,128]{2,1,0:T(8,128)(2,1)}, u32[]{:S(2)}) copy-start(bf16[1,128,128]{2,1,0:T(8,128)(2,1)} %basis_g.1) | copy-start | bytes 98308
  47.1 36.6 %copy-start.2 = (f32[1,1152]{1,0:T(1,128)S(1)}, f32[1,1152]{1,0:T(1,128)}, u32[]{:S(2)}) copy-start(f32[1,1152]{1,0:T(1,128)} %eig_a.1) | copy-start | bytes 13828
  47.1 36.6 %copy-start.3 = (f32[1,128]{1,0:T(1,128)S(1)}, f32[1,128]{1,0:T(1,128)}, u32[]{:S(2)}) copy-start(f32[1,128]{1,0:T(1,128)} %eig_g.1) | copy-start | bytes 1540
  47.2 4.6 %collective-permute-start.1 = (f32[14,8,128]{2,1,0:T(8,128)S(1)}, f32[14,8,128]{2,1,0:T(8,128)S(1)}, u32[]{:S(2)}, u32[]{:S(2)}) collective-permute-start(f32[14,8,128]{2,1,0:T(8,128)S(1)} %collect.1), channel_id=1, source_target_pairs={{0,1},{1,0},{2,3},{3,2},{4,5},{5,4},{6,7},{7,6},{8,9},{9,8},{10,11... | collective-permute-start | bytes 172040 | tf_op jit(solution)/shard_map/ppermute | solution.py:276
  51.8 8.6 %collective-permute-start.2 = (f32[14,8,128]{2,1,0:T(8,128)S(1)}, f32[14,8,128]{2,1,0:T(8,128)S(1)}, u32[]{:S(2)}, u32[]{:S(2)}) collective-permute-start(f32[14,8,128]{2,1,0:T(8,128)S(1)} %add.13), channel_id=1, source_target_pairs={{0,3},{1,2},{2,1},{3,0},{4,7},{5,6},{6,5},{7,4},{8,11},{9,10},{10,... | collective-permute-start | bytes 172040 | tf_op jit(solution)/shard_map/ppermute | solution.py:277
  56.4 6.1 %collective-permute-start.4 = (f32[14,8,128]{2,1,0:T(8,128)S(1)}, f32[14,8,128]{2,1,0:T(8,128)S(1)}, u32[]{:S(2)}, u32[]{:S(2)}) collective-permute-start(f32[14,8,128]{2,1,0:T(8,128)S(1)} %add.13), channel_id=1, source_target_pairs={{0,7},{1,6},{2,5},{3,4},{4,3},{5,2},{6,1},{7,0},{8,15},{9,14},{10,... | collective-permute-start | bytes 172040 | tf_op jit(solution)/shard_map/ppermute | solution.py:279
  60.1 2.5 %collective-permute-start.3 = (f32[14,8,128]{2,1,0:T(8,128)S(1)}, f32[14,8,128]{2,1,0:T(8,128)S(1)}, u32[]{:S(2)}, u32[]{:S(2)}) collective-permute-start(f32[14,8,128]{2,1,0:T(8,128)S(1)} %add.13), channel_id=1, source_target_pairs={{0,4},{4,0},{1,5},{5,1},{2,6},{6,2},{3,7},{7,3},{8,12},{12,8},{9,1... | collective-permute-start | bytes 172040 | tf_op jit(solution)/shard_map/ppermute | solution.py:272
  77.7 6.0 %collective-permute-start.5 = (f32[32,4,8,128]{3,2,1,0:T(8,128)S(1)}, f32[32,4,8,128]{3,2,1,0:T(8,128)S(1)}, u32[]{:S(2)}, u32[]{:S(2)}) collective-permute-start(f32[32,4,8,128]{3,2,1,0:T(8,128)S(1)} %all_to_all.11.got), channel_id=1, source_target_pairs={{0,4},{4,0},{1,5},{5,1},{2,6},{6,2},{3,7},{7,3},{8,12},{12,8},{9,1... | collective-permute-start | bytes 1572872 | tf_op jit(solution)/shard_map/ppermute | solution.py:272
where the time goes:
time: 86.4 us; the launch traced here: 86.1 us
  blocking collectives  44.6 us (52%)
  starting transfers between devices  19.4 us (22%)
  Pallas kernels  11.7 us (14%)
  waiting for transfers between devices  7.73 us (9%)
  between operations  1.33 us (2%)
  local copies, waits for them, and re-layouts  1.05 us (1%)
    all_to_all x1, blocking collectives, on_device(): met = lax.all_to_all(mine + swap_cores(theirs), CHIP_AXES, 0, 0, tiled=True)  30.2 us
    all_to_all x1, blocking collectives, on_device(): got = lax.all_to_all(send, CHIP_AXES, 0, 0, tiled=True)  14.4 us
    ppermute x3, starting transfers between devices, swap_cores(): return lax.ppermute(value, 'core', [(0, 1), (1, 0)])  8.06 us
    pallas_call x1, Pallas kernels, gram(): pl.pallas_call(gram_kernel, out_shape=(half, half), in_specs=[pl.BlockSpe...  7.45 us
    ppermute x1, starting transfers between devices, group_sums(): far = lax.ppermute(value, 'zh', [(i, i ^ 3) for i in range(4)])  4.61 us
    ppermute x3, waiting for transfers between devices, swap_cores(): return lax.ppermute(value, 'core', [(0, 1), (1, 0)])  4 us
    ppermute x1, starting transfers between devices, group_sums(): lax.ppermute(value, ('core', 'zh'), [(i, i ^ 7) for i in range(8)])  3.66 us
    ppermute x1, starting transfers between devices, group_sums(): value = value + lax.ppermute(value, 'zh', [(i, i ^ 1) for i in range(4)])  3.08 us
  transfers between devices with their start and end apart: 6, of which 4 were waited for; matrix products, arithmetic and copies ran while one was open for 0% of the time, Pallas kernels for 1%

commit v1 on v0

--- a/solution.py
+++ b/solution.py
@@ -3,7 +3,7 @@
 from jax import lax
 from jax.experimental import pallas as pl
 from jax.experimental.pallas import tpu as pltpu
-from jax.sharding import Mesh, PartitionSpec as P
+from jax.sharding import PartitionSpec as P
 
 DA, DG, ROWS = 1152, 128, 2048
 WIDTH = DA + DG
@@ -12,7 +12,11 @@
 HALF = BLOCKS // 2 + 1
 CHIPS, SLOTS, GRADS = 32, 14, 3
 LOW = SLOTS - GRADS
-CHIP_AXES = ("zl", "y", "xh", "xl")
+CHIP_GROUPS = [[2 * n + core for n in range(CHIPS)] for core in (0, 1)]
+FIRST = [[32 * zl + 8 * y + 2 * x for x in range(4)] for zl in range(2) for y in range(4)]
+FIRST += [[32 * zl + 8 * y + 2 * x + 1 for y in range(4)] for zl in range(2) for x in range(4)]
+SECOND = [[32 * zl + 8 * y + 2 * x for zl in range(2) for y in range(4)] for x in range(4)]
+SECOND += [[32 * zl + 8 * y + 2 * x + 1 for zl in range(2) for x in range(4)] for y in range(4)]
 HBM = pltpu.MemorySpace.HBM
 F32, BF16 = jnp.float32, jnp.bfloat16
 
@@ -40,14 +44,20 @@
 
 
 def position():
-    group = (lax.axis_index("zl") * 4 + lax.axis_index("y")) * 2 + lax.axis_index("xh")
-    return group, lax.axis_index("xl"), lax.axis_index("core")
+    dp = lax.axis_index("dp")
+    return lax.div(dp, 4), lax.rem(lax.div(dp, 2), 2), lax.rem(dp, 2)
+
+
+def ordered(core, chip):
+    zl, y, x = chip // 16, chip // 4 % 4, chip % 4
+    return (y, 4 * zl + x) if core else (x, 4 * zl + y)
 
 
 def products(part, z, zt, acc):
     depth = slice(PARTS[part], PARTS[part + 1])
 
     def put(place, tile):
+        place = place[:1] + ordered(*place[:2]) + place[2:]
         acc[place] = acc[place] + tile if part else tile
 
     for col0 in range(0, BLOCKS + 1, 2):
@@ -87,8 +97,8 @@
         )
         for copy in copies[k]:
             copy.start()
-    count, core = count_ref[0], lax.axis_index("core")
-    acc[1, :, SLOTS - 1, 4:8, :] = jnp.full((CHIPS, 4, 128), count.astype(F32))
+    count, core = count_ref[0], lax.rem(lax.axis_index("dp"), 2)
+    acc[1, :, :, SLOTS - 1, 4:8, :] = jnp.full((4, 8, 4, 128), count.astype(F32))
     for k in range(len(PARTS) - 1):
         for copy in copies[k]:
             copy.wait()
@@ -105,7 +115,7 @@
 
 
 def gram(patches, out_grads, counts):
-    half = jax.ShapeDtypeStruct((CHIPS, SLOTS, 8, 128), F32)
+    half = jax.ShapeDtypeStruct((4, 8, SLOTS, 8, 128), F32)
     return pl.pallas_call(
         gram_kernel,
         out_shape=(half, half),
@@ -114,7 +124,7 @@
         scratch_shapes=[
             pltpu.VMEM((ROWS, WIDTH), BF16),
             pltpu.VMEM((WIDTH, ROWS), BF16),
-            pltpu.VMEM((2, CHIPS, SLOTS, 8, 128), F32),
+            pltpu.VMEM((2, 4, 8, SLOTS, 8, 128), F32),
             pltpu.SemaphoreType.DMA((len(PARTS) - 1, 2)),
             pltpu.SemaphoreType.DMA((2,)),
         ],
@@ -126,7 +136,7 @@
 
 def collect_kernel(met, out):
     total = met[0]
-    for n in range(1, CHIPS):
+    for n in range(1, met.shape[0]):
         total = total + met[n]
     out[...] = total
 
@@ -134,7 +144,7 @@
 def collect(met):
     return pl.pallas_call(
         collect_kernel,
-        out_shape=jax.ShapeDtypeStruct((SLOTS, 8, 128), F32),
+        out_shape=jax.ShapeDtypeStruct(met.shape[1:], F32),
         compiler_params=pltpu.CompilerParams(vmem_limit_bytes=16 * 2**20),
         name="collect",
     )(met)
@@ -237,7 +247,7 @@
 
 
 def precond_kernel(got, other, total_ref, basis_a, basis_g, eig_a, eig_g, g_factor, precond):
-    core = lax.axis_index("core")
+    core = lax.rem(lax.axis_index("dp"), 2)
     total = total_ref[0:1, 0:1]
     shape = (16, 2, GRADS + 1, 8, 128)
     both = (got[...].reshape(shape), other[...].reshape(shape))
@@ -269,22 +279,27 @@
 
 
 def swap_cores(value):
-    return lax.ppermute(value, "core", [(0, 1), (1, 0)])
+    return lax.ppermute(value, "dp", [(i, i ^ 1) for i in range(64)])
 
 
 def group_sums(value):
-    value = value + lax.ppermute(value, "zh", [(i, i ^ 1) for i in range(4)])
-    far = lax.ppermute(value, "zh", [(i, i ^ 3) for i in range(4)])
+    value = value + lax.ppermute(value, "grp", [(i, i ^ 1) for i in range(4)])
+    far = lax.ppermute(value, "grp", [(i, i ^ 3) for i in range(4)])
     twin = swap_cores(value)
-    twin_far = lax.ppermute(value, ("core", "zh"), [(i, i ^ 7) for i in range(8)])
+    twin_far = lax.ppermute(value, ("dp", "grp"), [(i, i ^ 7) for i in range(256)])
     return value + far, twin + twin_far
+
+
+def exchange(value, groups):
+    return lax.all_to_all(value, "dp", 0, 0, axis_index_groups=groups, tiled=True)
 
 
 def on_device(patches, out_grads, counts, basis_a, basis_g, eig_a, eig_g):
     mine, theirs = gram(patches, out_grads, counts)
-    met = lax.all_to_all(mine + swap_cores(theirs), CHIP_AXES, 0, 0, tiled=True)
-    send, direct, total = spread(*group_sums(collect(met)))
-    got = lax.all_to_all(send, CHIP_AXES, 0, 0, tiled=True)
+    line = collect(exchange(mine + swap_cores(theirs), FIRST))
+    part = collect(exchange(line, SECOND))
+    send, direct, total = spread(*group_sums(part))
+    got = exchange(send, CHIP_GROUPS)
     other = swap_cores(got)
     a_factor = factor_rows(got, direct, total)
     g_factor, precond = precondition(got, other, total, basis_a, basis_g, eig_a, eig_g)
@@ -292,13 +307,12 @@
 
 
 def solution(mesh):
-    axes = ("zl", "y", "xh", "xl", "core", "zh")
-    finer = Mesh(mesh.devices.reshape(2, 4, 2, 2, 2, 4), axes)
-    placed = (P(None, axes, None), P(None, axes, None), P(axes), P(), P(), P(), P())
+    both = ("dp", "grp")
+    placed = (P(None, both, None), P(None, both, None), P(both), P(), P(), P(), P())
     return jax.shard_map(
         on_device,
-        mesh=finer,
+        mesh=mesh,
         in_specs=placed,
-        out_specs=(P(None, axes[:-1], None), P(), P()),
+        out_specs=(P(None, "dp", None), P(), P()),
         check_vma=False,
     )

time: 86.4 us -> 84.6 us (0.979)
  starting transfers between devices: 19.4 us -> 17.5 us
  waiting for transfers between devices: 7.73 us -> 9.18 us
  blocking collectives: 44.6 us -> 43.2 us
    ppermute x6, starting transfers between devices: 19.4 us -> 17.5 us  [the longest x3 7.47 us: swap_cores(): return lax.ppermute(value, 'dp', [(i, i ^ 1) for i in range(64)])]
    ppermute x6, waiting for transfers between devices: 7.73 us -> 9.18 us  [the longest x3 4 us: swap_cores(): return lax.ppermute(value, 'dp', [(i, i ^ 1) for i in range(64)])]
    all_to_all x2 -> x3, blocking collectives: 44.6 us -> 43.2 us  [exchange(): lax.all_to_all(value, 'dp', 0, 0, axis_index_groups=groups, tiled=True)]
where the time goes in v1:
time: 84.6 us; the launch traced here: 84.3 us
  blocking collectives  43.2 us (51%)
  starting transfers between devices  17.5 us (21%)
  Pallas kernels  11.7 us (14%)
  waiting for transfers between devices  9.18 us (11%)
  between operations  1.36 us (2%)
  local copies, waits for them, and re-layouts  1.06 us (1%)
    all_to_all x3, blocking collectives, exchange(): lax.all_to_all(value, 'dp', 0, 0, axis_index_groups=groups, tiled=True)  43.2 us
    ppermute x3, starting transfers between devices, swap_cores(): return lax.ppermute(value, 'dp', [(i, i ^ 1) for i in range(64)])  7.47 us
    pallas_call x1, Pallas kernels, gram(): pl.pallas_call(gram_kernel, out_shape=(half, half), in_specs=[pl.BlockSpe...  7.45 us
    ppermute x3, waiting for transfers between devices, swap_cores(): return lax.ppermute(value, 'dp', [(i, i ^ 1) for i in range(64)])  4 us
    ppermute x1, starting transfers between devices, group_sums(): far = lax.ppermute(value, 'grp', [(i, i ^ 3) for i in range(4)])  3.98 us
    ppermute x1, starting transfers between devices, group_sums(): value = value + lax.ppermute(value, 'grp', [(i, i ^ 1) for i in range(4)])  3.08 us
    ppermute x1, waiting for transfers between devices, group_sums(): lax.ppermute(value, ('dp', 'grp'), [(i, i ^ 7) for i in range(256)])  2.99 us
    ppermute x1, starting transfers between devices, group_sums(): lax.ppermute(value, ('dp', 'grp'), [(i, i ^ 7) for i in range(256)])  2.96 us
  transfers between devices with their start and end apart: 6, of which 4 were waited for; matrix products, arithmetic and copies ran while one was open for 0% of the time, Pallas kernels for 1%

profile of v1, /device:TPU:1, one launch (start us, length us, event | category | flops | bytes accessed | tf_op | source)
XLA Modules:
  0.0 84.3 jit_solution(927234167408658823)
XLA Ops:
  1.3 0.0 copy-start.4
  1.3 1.0 %copy-done.4 = bf16[1,2048,128]{2,1,0:T(8,128)(2,1)S(1)} copy-done((bf16[1,2048,128]{2,1,0:T(8,128)(2,1)S(1)}, bf16[1,2048,128]{2,1,0:T(8,128)(2,1)}, u32[]{:S(2)}) %copy-start.4) | copy-done | bytes 524312
  2.3 7.4 %gram.1 = (f32[4,8,14,8,128]{4,3,2,1,0:T(8,128)S(1)}, f32[4,8,14,8,128]{4,3,2,1,0:T(8,128)S(1)}) custom-call(s32[1]{0:T(128)S(6)} %copy.10.count_ref, bf16[1,2048,1152]{2,1,0:T(8,128)(2,1)} %x_hbm.1, bf16[1,2048,128]{2,1,0:T(8,128)(2,1)S(1)} %copy-done.4), custom_call_target="tpu_custom_call" | custom-call | flops 6710886400 | bytes 10485760 | tf_op jit(solution)/shard_map/gram/pallas_call | solution.py:119
  9.8 3.3 %collective-permute-start = (f32[4,8,14,8,128]{4,3,2,1,0:T(8,128)S(1)}, f32[4,8,14,8,128]{4,3,2,1,0:T(8,128)S(1)}, u32[]{:S(2)}, u32[]{:S(2)}) collective-permute-start(f32[4,8,14,8,128]{4,3,2,1,0:T(8,128)S(1)} %get-tuple-element.11), channel_id=1, source_target_pairs={{0,4},{4,0},{8,12},{12,8},{16,20},{20,16},{24,28},{28,24},{32,36},... | collective-permute-start | bytes 5505032 | tf_op jit(solution)/shard_map/ppermute | solution.py:282
  13.1 3.4 %collective-permute-done = f32[4,8,14,8,128]{4,3,2,1,0:T(8,128)S(1)} collective-permute-done((f32[4,8,14,8,128]{4,3,2,1,0:T(8,128)S(1)}, f32[4,8,14,8,128]{4,3,2,1,0:T(8,128)S(1)}, u32[]{:S(2)}, u32[]{:S(2)}) %collective-permute-start) | collective-permute-done | bytes 1835040 | tf_op jit(solution)/shard_map/ppermute | solution.py:282
  16.5 0.3 add.12
  16.8 16.7 %all_to_all.15.met = f32[4,8,14,8,128]{4,3,2,1,0:T(8,128)S(1)} all-to-all(f32[4,8,14,8,128]{4,3,2,1,0:T(8,128)S(1)} %add.12), channel_id=1, replica_groups={{0,8,16,24},{32,40,48,56},{64,72,80,88},{96,104,112,120},{128,136,144,1..., dimensions={0} | all-to-all | bytes 3670016 | tf_op jit(solution)/shard_map/all_to_all | solution.py:294
  33.5 0.1 collect.2
  33.6 0.0 copy-start
  33.6 0.0 copy-start.1
  33.6 0.0 copy-start.2
  33.6 0.0 copy-start.3
  33.7 13.5 %all_to_all.16.met = f32[8,14,8,128]{3,2,1,0:T(8,128)S(1)} all-to-all(f32[8,14,8,128]{3,2,1,0:T(8,128)S(1)} %collect.2), channel_id=1, replica_groups={{0,32,64,96,128,160,192,224},{8,40,72,104,136,168,200,232},{16,48,80,11..., dimensions={0} | all-to-all | bytes 917504 | tf_op jit(solution)/shard_map/all_to_all | solution.py:294
  47.2 3.1 %collective-permute-start.1 = (f32[14,8,128]{2,1,0:T(8,128)S(1)}, f32[14,8,128]{2,1,0:T(8,128)S(1)}, u32[]{:S(2)}, u32[]{:S(2)}) collective-permute-start(f32[14,8,128]{2,1,0:T(8,128)S(1)} %collect.3), channel_id=1, source_target_pairs={{0,1},{1,0},{2,3},{3,2},{4,5},{5,4},{6,7},{7,6},{8,9},{9,8},{10,11... | collective-permute-start | bytes 172040 | tf_op jit(solution)/shard_map/ppermute | solution.py:286
  50.3 2.2 %collective-permute-done.1 = f32[14,8,128]{2,1,0:T(8,128)S(1)} collective-permute-done((f32[14,8,128]{2,1,0:T(8,128)S(1)}, f32[14,8,128]{2,1,0:T(8,128)S(1)}, u32[]{:S(2)}, u32[]{:S(2)}) %collective-permute-start.1) | collective-permute-done | bytes 57376 | tf_op jit(solution)/shard_map/ppermute | solution.py:286
  52.5 4.0 %collective-permute-start.2 = (f32[14,8,128]{2,1,0:T(8,128)S(1)}, f32[14,8,128]{2,1,0:T(8,128)S(1)}, u32[]{:S(2)}, u32[]{:S(2)}) collective-permute-start(f32[14,8,128]{2,1,0:T(8,128)S(1)} %add.13), channel_id=1, source_target_pairs={{0,3},{1,2},{2,1},{3,0},{4,7},{5,6},{6,5},{7,4},{8,11},{9,10},{10,... | collective-permute-start | bytes 172040 | tf_op jit(solution)/shard_map/ppermute | solution.py:287
  56.4 3.0 %collective-permute-start.4 = (f32[14,8,128]{2,1,0:T(8,128)S(1)}, f32[14,8,128]{2,1,0:T(8,128)S(1)}, u32[]{:S(2)}, u32[]{:S(2)}) collective-permute-start(f32[14,8,128]{2,1,0:T(8,128)S(1)} %add.13), channel_id=1, source_target_pairs={{0,7},{1,6},{2,5},{3,4},{4,3},{5,2},{6,1},{7,0},{8,15},{9,14},{10,... | collective-permute-start | bytes 172040 | tf_op jit(solution)/shard_map/ppermute | solution.py:289
  59.4 0.3 collective-permute-start.3
  59.7 0.0 collective-permute-done.2
  59.7 3.0 %collective-permute-done.4 = f32[14,8,128]{2,1,0:T(8,128)S(1)} collective-permute-done((f32[14,8,128]{2,1,0:T(8,128)S(1)}, f32[14,8,128]{2,1,0:T(8,128)S(1)}, u32[]{:S(2)}, u32[]{:S(2)}) %collective-permute-start.4) | collective-permute-done | bytes 57376 | tf_op jit(solution)/shard_map/ppermute | solution.py:289
  62.7 0.0 collective-permute-done.3
  62.7 0.7 spread.1
  63.4 13.0 %all_to_all.17.got = f32[32,4,8,128]{3,2,1,0:T(8,128)S(1)} all-to-all(f32[32,4,8,128]{3,2,1,0:T(8,128)S(1)} %get-tuple-element.12), channel_id=1, replica_groups={{0,8,16,24,32,40,48,56,64,72,80,88,96,104,112,120,128,136,144,152,160,1..., dimensions={0} | all-to-all | bytes 1048576 | tf_op jit(solution)/shard_map/all_to_all | solution.py:294
  76.4 3.8 %collective-permute-start.5 = (f32[32,4,8,128]{3,2,1,0:T(8,128)S(1)}, f32[32,4,8,128]{3,2,1,0:T(8,128)S(1)}, u32[]{:S(2)}, u32[]{:S(2)}) collective-permute-start(f32[32,4,8,128]{3,2,1,0:T(8,128)S(1)} %all_to_all.17.got), channel_id=1, source_target_pairs={{0,4},{4,0},{8,12},{12,8},{16,20},{20,16},{24,28},{28,24},{32,36},... | collective-permute-start | bytes 1572872 | tf_op jit(solution)/shard_map/ppermute | solution.py:282
  80.3 0.9 %factor_rows.1 = f32[18,1,1152]{2,1,0:T(1,128)} custom-call(f32[32,4,8,128]{3,2,1,0:T(8,128)S(1)} %all_to_all.17.got, f32[9,40,128]{2,1,0:T(8,128)S(1)} %get-tuple-element.13.direct, f32[8,128]{1,0:T(8,128)S(1)} %get-tuple-element.14.total_ref), custom_call_target="tpu_custom_call" | custom-call | flops 1000000 | bytes 1048576 | tf_op jit(solution)/shard_map/factor_rows/pallas_call | solution.py:237
  81.2 0.6 collective-permute-done.5.other
  81.8 0.0 copy-done
  81.8 0.0 copy-done.1
  81.8 0.0 copy-done.2
  81.8 0.0 copy-done.3
  81.8 2.5 %precondition.1 = (f32[1,128,128]{2,1,0:T(8,128)}, f32[1,128,1152]{2,1,0:T(8,128)}) custom-call(f32[32,4,8,128]{3,2,1,0:T(8,128)S(1)} %all_to_all.17.got, f32[32,4,8,128]{3,2,1,0:T(8,128)S(1)} %collective-permute-done.5.other, f32[8,128]{1,0:T(8,128)S(1)} %get-tuple-element.14.total_ref, bf16[1,1152,1152]{2,1,0:T(8,128)(2,1)S(1)} %copy-done, ...), custom_call_target="tpu_custom_call" | custom-call | tf_op jit(solution)/shard_map/precondition/pallas_call | solution.py:272
  (4 shorter events, 0.1 us)
Async XLA Ops:
  1.3 1.0 %copy-start.4 = (bf16[1,2048,128]{2,1,0:T(8,128)(2,1)S(1)}, bf16[1,2048,128]{2,1,0:T(8,128)(2,1)}, u32[]{:S(2)}) copy-start(bf16[1,2048,128]{2,1,0:T(8,128)(2,1)} %y_hbm.1) | copy-start | bytes 1572868
  9.8 6.7 %collective-permute-start = (f32[4,8,14,8,128]{4,3,2,1,0:T(8,128)S(1)}, f32[4,8,14,8,128]{4,3,2,1,0:T(8,128)S(1)}, u32[]{:S(2)}, u32[]{:S(2)}) collective-permute-start(f32[4,8,14,8,128]{4,3,2,1,0:T(8,128)S(1)} %get-tuple-element.11), channel_id=1, source_target_pairs={{0,4},{4,0},{8,12},{12,8},{16,20},{20,16},{24,28},{28,24},{32,36},... | collective-permute-start | bytes 5505032 | tf_op jit(solution)/shard_map/ppermute | solution.py:282
  33.6 48.2 %copy-start = (bf16[1,1152,1152]{2,1,0:T(8,128)(2,1)S(1)}, bf16[1,1152,1152]{2,1,0:T(8,128)(2,1)}, u32[]{:S(2)}) copy-start(bf16[1,1152,1152]{2,1,0:T(8,128)(2,1)} %basis_a.1) | copy-start | bytes 7962628
  33.6 48.2 %copy-start.1 = (bf16[1,128,128]{2,1,0:T(8,128)(2,1)S(1)}, bf16[1,128,128]{2,1,0:T(8,128)(2,1)}, u32[]{:S(2)}) copy-start(bf16[1,128,128]{2,1,0:T(8,128)(2,1)} %basis_g.1) | copy-start | bytes 98308
  33.6 48.2 %copy-start.2 = (f32[1,1152]{1,0:T(1,128)S(1)}, f32[1,1152]{1,0:T(1,128)}, u32[]{:S(2)}) copy-start(f32[1,1152]{1,0:T(1,128)} %eig_a.1) | copy-start | bytes 13828
  33.6 48.2 %copy-start.3 = (f32[1,128]{1,0:T(1,128)S(1)}, f32[1,128]{1,0:T(1,128)}, u32[]{:S(2)}) copy-start(f32[1,128]{1,0:T(1,128)} %eig_g.1) | copy-start | bytes 1540
  47.2 5.3 %collective-permute-start.1 = (f32[14,8,128]{2,1,0:T(8,128)S(1)}, f32[14,8,128]{2,1,0:T(8,128)S(1)}, u32[]{:S(2)}, u32[]{:S(2)}) collective-permute-start(f32[14,8,128]{2,1,0:T(8,128)S(1)} %collect.3), channel_id=1, source_target_pairs={{0,1},{1,0},{2,3},{3,2},{4,5},{5,4},{6,7},{7,6},{8,9},{9,8},{10,11... | collective-permute-start | bytes 172040 | tf_op jit(solution)/shard_map/ppermute | solution.py:286
  52.5 7.2 %collective-permute-start.2 = (f32[14,8,128]{2,1,0:T(8,128)S(1)}, f32[14,8,128]{2,1,0:T(8,128)S(1)}, u32[]{:S(2)}, u32[]{:S(2)}) collective-permute-start(f32[14,8,128]{2,1,0:T(8,128)S(1)} %add.13), channel_id=1, source_target_pairs={{0,3},{1,2},{2,1},{3,0},{4,7},{5,6},{6,5},{7,4},{8,11},{9,10},{10,... | collective-permute-start | bytes 172040 | tf_op jit(solution)/shard_map/ppermute | solution.py:287
  56.4 6.3 %collective-permute-start.4 = (f32[14,8,128]{2,1,0:T(8,128)S(1)}, f32[14,8,128]{2,1,0:T(8,128)S(1)}, u32[]{:S(2)}, u32[]{:S(2)}) collective-permute-start(f32[14,8,128]{2,1,0:T(8,128)S(1)} %add.13), channel_id=1, source_target_pairs={{0,7},{1,6},{2,5},{3,4},{4,3},{5,2},{6,1},{7,0},{8,15},{9,14},{10,... | collective-permute-start | bytes 172040 | tf_op jit(solution)/shard_map/ppermute | solution.py:289
  59.4 3.3 %collective-permute-start.3 = (f32[14,8,128]{2,1,0:T(8,128)S(1)}, f32[14,8,128]{2,1,0:T(8,128)S(1)}, u32[]{:S(2)}, u32[]{:S(2)}) collective-permute-start(f32[14,8,128]{2,1,0:T(8,128)S(1)} %add.13), channel_id=1, source_target_pairs={{0,4},{4,0},{8,12},{12,8},{16,20},{20,16},{24,28},{28,24},{32,36},... | collective-permute-start | bytes 172040 | tf_op jit(solution)/shard_map/ppermute | solution.py:282
  76.4 5.4 %collective-permute-start.5 = (f32[32,4,8,128]{3,2,1,0:T(8,128)S(1)}, f32[32,4,8,128]{3,2,1,0:T(8,128)S(1)}, u32[]{:S(2)}, u32[]{:S(2)}) collective-permute-start(f32[32,4,8,128]{3,2,1,0:T(8,128)S(1)} %all_to_all.17.got), channel_id=1, source_target_pairs={{0,4},{4,0},{8,12},{12,8},{16,20},{20,16},{24,28},{28,24},{32,36},... | collective-permute-start | bytes 1572872 | tf_op jit(solution)/shard_map/ppermute | solution.py:282

commit v2 on v1

--- a/solution.py
+++ b/solution.py
@@ -282,12 +282,10 @@
     return lax.ppermute(value, "dp", [(i, i ^ 1) for i in range(64)])
 
 
-def group_sums(value):
-    value = value + lax.ppermute(value, "grp", [(i, i ^ 1) for i in range(4)])
-    far = lax.ppermute(value, "grp", [(i, i ^ 3) for i in range(4)])
-    twin = swap_cores(value)
-    twin_far = lax.ppermute(value, ("dp", "grp"), [(i, i ^ 7) for i in range(256)])
-    return value + far, twin + twin_far
+def group_sum(value):
+    for k in (1, 3):
+        value = value + lax.ppermute(value, "grp", [(i, i ^ k) for i in range(4)])
+    return value
 
 
 def exchange(value, groups):
@@ -297,8 +295,8 @@
 def on_device(patches, out_grads, counts, basis_a, basis_g, eig_a, eig_g):
     mine, theirs = gram(patches, out_grads, counts)
     line = collect(exchange(mine + swap_cores(theirs), FIRST))
-    part = collect(exchange(line, SECOND))
-    send, direct, total = spread(*group_sums(part))
+    done = group_sum(collect(exchange(line, SECOND)))
+    send, direct, total = spread(done, swap_cores(done))
     got = exchange(send, CHIP_GROUPS)
     other = swap_cores(got)
     a_factor = factor_rows(got, direct, total)

time: 84.6 us -> 84.1 us (level)
  starting transfers between devices: 17.5 us -> 16.5 us
  blocking collectives: 43.2 us -> 44.1 us
    ppermute x3 -> x2, starting transfers between devices: 10 us -> 7.05 us  [group_sum(): value = value + lax.ppermute(value, 'grp', [(i, i ^ k) for i in range(4)])]
    ppermute x3, starting transfers between devices: 7.47 us -> 9.44 us  [swap_cores(): return lax.ppermute(value, 'dp', [(i, i ^ 1) for i in range(64)])]
    ppermute x3 -> x2, waiting for transfers between devices: 5.17 us -> 3.92 us  [group_sum(): value = value + lax.ppermute(value, 'grp', [(i, i ^ k) for i in range(4)])]
    ppermute x3, waiting for transfers between devices: 4 us -> 4.89 us  [swap_cores(): return lax.ppermute(value, 'dp', [(i, i ^ 1) for i in range(64)])]
    all_to_all x3, blocking collectives: 43.2 us -> 44.1 us  [exchange(): lax.all_to_all(value, 'dp', 0, 0, axis_index_groups=groups, tiled=True)]
  transfers between devices with their start and end apart: 6 -> 5, of which waited for: 4 -> 5; matrix products, arithmetic and copies ran while one was open for 0% -> 0% of each run, Pallas kernels for 1% -> 1%
where the time goes in v2:
time: 84.1 us; the launch traced here: 83.8 us
  blocking collectives  44.1 us (52%)
  starting transfers between devices  16.5 us (20%)
  Pallas kernels  11.7 us (14%)
  waiting for transfers between devices  8.81 us (10%)
  between operations  1.35 us (2%)
  local copies, waits for them, and re-layouts  1.06 us (1%)
    all_to_all x3, blocking collectives, exchange(): lax.all_to_all(value, 'dp', 0, 0, axis_index_groups=groups, tiled=True)  44.1 us
    ppermute x3, starting transfers between devices, swap_cores(): return lax.ppermute(value, 'dp', [(i, i ^ 1) for i in range(64)])  9.44 us
    pallas_call x1, Pallas kernels, gram(): pl.pallas_call(gram_kernel, out_shape=(half, half), in_specs=[pl.BlockSpe...  7.45 us
    ppermute x2, starting transfers between devices, group_sum(): value = value + lax.ppermute(value, 'grp', [(i, i ^ k) for i in range(4)])  7.05 us
    ppermute x3, waiting for transfers between devices, swap_cores(): return lax.ppermute(value, 'dp', [(i, i ^ 1) for i in range(64)])  4.89 us
    ppermute x2, waiting for transfers between devices, group_sum(): value = value + lax.ppermute(value, 'grp', [(i, i ^ k) for i in range(4)])  3.92 us
    pallas_call x1, Pallas kernels, precondition(): pl.pallas_call(precond_kernel, out_shape=(jax.ShapeDtypeStruct((1, DG, DG...  2.51 us
  transfers between devices with their start and end apart: 5, of which 5 were waited for; matrix products, arithmetic and copies ran while one was open for 0% of the time, Pallas kernels for 1%

profile of v2, /device:TPU:1, one launch (start us, length us, event | category | flops | bytes accessed | tf_op | source)
XLA Modules:
  0.0 83.8 jit_solution(1316931039187746374)
XLA Ops:
  1.3 0.0 copy-start.4
  1.3 1.0 %copy-done.4 = bf16[1,2048,128]{2,1,0:T(8,128)(2,1)S(1)} copy-done((bf16[1,2048,128]{2,1,0:T(8,128)(2,1)S(1)}, bf16[1,2048,128]{2,1,0:T(8,128)(2,1)}, u32[]{:S(2)}) %copy-start.4) | copy-done | bytes 524312
  2.3 7.4 %gram.1 = (f32[4,8,14,8,128]{4,3,2,1,0:T(8,128)S(1)}, f32[4,8,14,8,128]{4,3,2,1,0:T(8,128)S(1)}) custom-call(s32[1]{0:T(128)S(6)} %copy.10.count_ref, bf16[1,2048,1152]{2,1,0:T(8,128)(2,1)} %x_hbm.1, bf16[1,2048,128]{2,1,0:T(8,128)(2,1)S(1)} %copy-done.4), custom_call_target="tpu_custom_call" | custom-call | flops 6710886400 | bytes 10485760 | tf_op jit(solution)/shard_map/gram/pallas_call | solution.py:119
  9.8 3.3 %collective-permute-start = (f32[4,8,14,8,128]{4,3,2,1,0:T(8,128)S(1)}, f32[4,8,14,8,128]{4,3,2,1,0:T(8,128)S(1)}, u32[]{:S(2)}, u32[]{:S(2)}) collective-permute-start(f32[4,8,14,8,128]{4,3,2,1,0:T(8,128)S(1)} %get-tuple-element.11), channel_id=1, source_target_pairs={{0,4},{4,0},{8,12},{12,8},{16,20},{20,16},{24,28},{28,24},{32,36},... | collective-permute-start | bytes 5505032 | tf_op jit(solution)/shard_map/ppermute | solution.py:282
  13.1 3.4 %collective-permute-done = f32[4,8,14,8,128]{4,3,2,1,0:T(8,128)S(1)} collective-permute-done((f32[4,8,14,8,128]{4,3,2,1,0:T(8,128)S(1)}, f32[4,8,14,8,128]{4,3,2,1,0:T(8,128)S(1)}, u32[]{:S(2)}, u32[]{:S(2)}) %collective-permute-start) | collective-permute-done | bytes 1835040 | tf_op jit(solution)/shard_map/ppermute | solution.py:282
  16.5 0.3 add.9
  16.8 16.7 %all_to_all.15.met = f32[4,8,14,8,128]{4,3,2,1,0:T(8,128)S(1)} all-to-all(f32[4,8,14,8,128]{4,3,2,1,0:T(8,128)S(1)} %add.9), channel_id=1, replica_groups={{0,8,16,24},{32,40,48,56},{64,72,80,88},{96,104,112,120},{128,136,144,1..., dimensions={0} | all-to-all | bytes 3670016 | tf_op jit(solution)/shard_map/all_to_all | solution.py:292
  33.5 0.1 collect.2
  33.6 0.0 copy-start
  33.6 0.0 copy-start.1
  33.6 0.0 copy-start.2
  33.6 0.0 copy-start.3
  33.7 13.5 %all_to_all.16.met = f32[8,14,8,128]{3,2,1,0:T(8,128)S(1)} all-to-all(f32[8,14,8,128]{3,2,1,0:T(8,128)S(1)} %collect.2), channel_id=1, replica_groups={{0,32,64,96,128,160,192,224},{8,40,72,104,136,168,200,232},{16,48,80,11..., dimensions={0} | all-to-all | bytes 917504 | tf_op jit(solution)/shard_map/all_to_all | solution.py:292
  47.2 3.1 %collective-permute-start.1 = (f32[14,8,128]{2,1,0:T(8,128)S(1)}, f32[14,8,128]{2,1,0:T(8,128)S(1)}, u32[]{:S(2)}, u32[]{:S(2)}) collective-permute-start(f32[14,8,128]{2,1,0:T(8,128)S(1)} %collect.3), channel_id=1, source_target_pairs={{0,1},{1,0},{2,3},{3,2},{4,5},{5,4},{6,7},{7,6},{8,9},{9,8},{10,11... | collective-permute-start | bytes 172040 | tf_op jit(solution)/shard_map/ppermute | solution.py:287
  50.3 2.2 %collective-permute-done.1 = f32[14,8,128]{2,1,0:T(8,128)S(1)} collective-permute-done((f32[14,8,128]{2,1,0:T(8,128)S(1)}, f32[14,8,128]{2,1,0:T(8,128)S(1)}, u32[]{:S(2)}, u32[]{:S(2)}) %collective-permute-start.1) | collective-permute-done | bytes 57376 | tf_op jit(solution)/shard_map/ppermute | solution.py:287
  52.5 4.0 %collective-permute-start.2 = (f32[14,8,128]{2,1,0:T(8,128)S(1)}, f32[14,8,128]{2,1,0:T(8,128)S(1)}, u32[]{:S(2)}, u32[]{:S(2)}) collective-permute-start(f32[14,8,128]{2,1,0:T(8,128)S(1)} %add.10), channel_id=1, source_target_pairs={{0,3},{1,2},{2,1},{3,0},{4,7},{5,6},{6,5},{7,4},{8,11},{9,10},{10,... | collective-permute-start | bytes 172040 | tf_op jit(solution)/shard_map/ppermute | solution.py:287
  56.4 1.7 %collective-permute-done.2 = f32[14,8,128]{2,1,0:T(8,128)S(1)} collective-permute-done((f32[14,8,128]{2,1,0:T(8,128)S(1)}, f32[14,8,128]{2,1,0:T(8,128)S(1)}, u32[]{:S(2)}, u32[]{:S(2)}) %collective-permute-start.2) | collective-permute-done | bytes 57376 | tf_op jit(solution)/shard_map/ppermute | solution.py:287
  58.2 3.9 %collective-permute-start.3 = (f32[14,8,128]{2,1,0:T(8,128)S(1)}, f32[14,8,128]{2,1,0:T(8,128)S(1)}, u32[]{:S(2)}, u32[]{:S(2)}) collective-permute-start(f32[14,8,128]{2,1,0:T(8,128)S(1)} %add.11.done), channel_id=1, source_target_pairs={{0,4},{4,0},{8,12},{12,8},{16,20},{20,16},{24,28},{28,24},{32,36},... | collective-permute-start | bytes 172040 | tf_op jit(solution)/shard_map/ppermute | solution.py:282
  62.1 0.9 %collective-permute-done.3.twin = f32[14,8,128]{2,1,0:T(8,128)S(1)} collective-permute-done((f32[14,8,128]{2,1,0:T(8,128)S(1)}, f32[14,8,128]{2,1,0:T(8,128)S(1)}, u32[]{:S(2)}, u32[]{:S(2)}) %collective-permute-start.3) | collective-permute-done | bytes 57376 | tf_op jit(solution)/shard_map/ppermute | solution.py:282
  63.0 0.7 spread.1
  63.6 13.9 %all_to_all.17.got = f32[32,4,8,128]{3,2,1,0:T(8,128)S(1)} all-to-all(f32[32,4,8,128]{3,2,1,0:T(8,128)S(1)} %get-tuple-element.12), channel_id=1, replica_groups={{0,8,16,24,32,40,48,56,64,72,80,88,96,104,112,120,128,136,144,152,160,1..., dimensions={0} | all-to-all | bytes 1048576 | tf_op jit(solution)/shard_map/all_to_all | solution.py:292
  77.6 2.2 %collective-permute-start.4 = (f32[32,4,8,128]{3,2,1,0:T(8,128)S(1)}, f32[32,4,8,128]{3,2,1,0:T(8,128)S(1)}, u32[]{:S(2)}, u32[]{:S(2)}) collective-permute-start(f32[32,4,8,128]{3,2,1,0:T(8,128)S(1)} %all_to_all.17.got), channel_id=1, source_target_pairs={{0,4},{4,0},{8,12},{12,8},{16,20},{20,16},{24,28},{28,24},{32,36},... | collective-permute-start | bytes 1572872 | tf_op jit(solution)/shard_map/ppermute | solution.py:282
  79.8 0.9 %factor_rows.1 = f32[18,1,1152]{2,1,0:T(1,128)} custom-call(f32[32,4,8,128]{3,2,1,0:T(8,128)S(1)} %all_to_all.17.got, f32[9,40,128]{2,1,0:T(8,128)S(1)} %get-tuple-element.13.direct, f32[8,128]{1,0:T(8,128)S(1)} %get-tuple-element.14.total_ref), custom_call_target="tpu_custom_call" | custom-call | flops 1000000 | bytes 1048576 | tf_op jit(solution)/shard_map/factor_rows/pallas_call | solution.py:237
  80.7 0.6 collective-permute-done.4.other
  81.3 0.0 copy-done
  81.3 0.0 copy-done.1
  81.3 0.0 copy-done.2
  81.3 0.0 copy-done.3
  81.3 2.5 %precondition.1 = (f32[1,128,128]{2,1,0:T(8,128)}, f32[1,128,1152]{2,1,0:T(8,128)}) custom-call(f32[32,4,8,128]{3,2,1,0:T(8,128)S(1)} %all_to_all.17.got, f32[32,4,8,128]{3,2,1,0:T(8,128)S(1)} %collective-permute-done.4.other, f32[8,128]{1,0:T(8,128)S(1)} %get-tuple-element.14.total_ref, bf16[1,1152,1152]{2,1,0:T(8,128)(2,1)S(1)} %copy-done, ...), custom_call_target="tpu_custom_call" | custom-call | tf_op jit(solution)/shard_map/precondition/pallas_call | solution.py:272
  (3 shorter events, 0.0 us)
Async XLA Ops:
  1.3 1.0 %copy-start.4 = (bf16[1,2048,128]{2,1,0:T(8,128)(2,1)S(1)}, bf16[1,2048,128]{2,1,0:T(8,128)(2,1)}, u32[]{:S(2)}) copy-start(bf16[1,2048,128]{2,1,0:T(8,128)(2,1)} %y_hbm.1) | copy-start | bytes 1572868
  9.8 6.7 %collective-permute-start = (f32[4,8,14,8,128]{4,3,2,1,0:T(8,128)S(1)}, f32[4,8,14,8,128]{4,3,2,1,0:T(8,128)S(1)}, u32[]{:S(2)}, u32[]{:S(2)}) collective-permute-start(f32[4,8,14,8,128]{4,3,2,1,0:T(8,128)S(1)} %get-tuple-element.11), channel_id=1, source_target_pairs={{0,4},{4,0},{8,12},{12,8},{16,20},{20,16},{24,28},{28,24},{32,36},... | collective-permute-start | bytes 5505032 | tf_op jit(solution)/shard_map/ppermute | solution.py:282
  33.6 47.7 %copy-start = (bf16[1,1152,1152]{2,1,0:T(8,128)(2,1)S(1)}, bf16[1,1152,1152]{2,1,0:T(8,128)(2,1)}, u32[]{:S(2)}) copy-start(bf16[1,1152,1152]{2,1,0:T(8,128)(2,1)} %basis_a.1) | copy-start | bytes 7962628
  33.6 47.7 %copy-start.1 = (bf16[1,128,128]{2,1,0:T(8,128)(2,1)S(1)}, bf16[1,128,128]{2,1,0:T(8,128)(2,1)}, u32[]{:S(2)}) copy-start(bf16[1,128,128]{2,1,0:T(8,128)(2,1)} %basis_g.1) | copy-start | bytes 98308
  33.6 47.7 %copy-start.2 = (f32[1,1152]{1,0:T(1,128)S(1)}, f32[1,1152]{1,0:T(1,128)}, u32[]{:S(2)}) copy-start(f32[1,1152]{1,0:T(1,128)} %eig_a.1) | copy-start | bytes 13828
  33.6 47.7 %copy-start.3 = (f32[1,128]{1,0:T(1,128)S(1)}, f32[1,128]{1,0:T(1,128)}, u32[]{:S(2)}) copy-start(f32[1,128]{1,0:T(1,128)} %eig_g.1) | copy-start | bytes 1540
  47.2 5.3 %collective-permute-start.1 = (f32[14,8,128]{2,1,0:T(8,128)S(1)}, f32[14,8,128]{2,1,0:T(8,128)S(1)}, u32[]{:S(2)}, u32[]{:S(2)}) collective-permute-start(f32[14,8,128]{2,1,0:T(8,128)S(1)} %collect.3), channel_id=1, source_target_pairs={{0,1},{1,0},{2,3},{3,2},{4,5},{5,4},{6,7},{7,6},{8,9},{9,8},{10,11... | collective-permute-start | bytes 172040 | tf_op jit(solution)/shard_map/ppermute | solution.py:287
  52.5 5.7 %collective-permute-start.2 = (f32[14,8,128]{2,1,0:T(8,128)S(1)}, f32[14,8,128]{2,1,0:T(8,128)S(1)}, u32[]{:S(2)}, u32[]{:S(2)}) collective-permute-start(f32[14,8,128]{2,1,0:T(8,128)S(1)} %add.10), channel_id=1, source_target_pairs={{0,3},{1,2},{2,1},{3,0},{4,7},{5,6},{6,5},{7,4},{8,11},{9,10},{10,... | collective-permute-start | bytes 172040 | tf_op jit(solution)/shard_map/ppermute | solution.py:287
  58.2 4.8 %collective-permute-start.3 = (f32[14,8,128]{2,1,0:T(8,128)S(1)}, f32[14,8,128]{2,1,0:T(8,128)S(1)}, u32[]{:S(2)}, u32[]{:S(2)}) collective-permute-start(f32[14,8,128]{2,1,0:T(8,128)S(1)} %add.11.done), channel_id=1, source_target_pairs={{0,4},{4,0},{8,12},{12,8},{16,20},{20,16},{24,28},{28,24},{32,36},... | collective-permute-start | bytes 172040 | tf_op jit(solution)/shard_map/ppermute | solution.py:282
  77.6 3.8 %collective-permute-start.4 = (f32[32,4,8,128]{3,2,1,0:T(8,128)S(1)}, f32[32,4,8,128]{3,2,1,0:T(8,128)S(1)}, u32[]{:S(2)}, u32[]{:S(2)}) collective-permute-start(f32[32,4,8,128]{3,2,1,0:T(8,128)S(1)} %all_to_all.17.got), channel_id=1, source_target_pairs={{0,4},{4,0},{8,12},{12,8},{16,20},{20,16},{24,28},{28,24},{32,36},... | collective-permute-start | bytes 1572872 | tf_op jit(solution)/shard_map/ppermute | solution.py:282

commit v3 on v2

--- a/solution.py
+++ b/solution.py
@@ -131,7 +131,7 @@
         compiler_params=pltpu.CompilerParams(vmem_limit_bytes=48 * 2**20),
         cost_estimate=pl.CostEstimate(flops=2 * ROWS * WIDTH * WIDTH, bytes_accessed=10 * 2**20, transcendentals=0),
         name="gram",
-    )(counts, patches, out_grads)
+    )(counts, *(pltpu.with_memory_space_constraint(v, HBM) for v in (patches, out_grads)))
 
 
 def collect_kernel(met, out):

time: 84.1 us -> 83 us (0.987)
  local copies, waits for them, and re-layouts: 1.06 us -> 0.03 us
    unnamed x10 -> x8, local copies, waits for them, and re-layouts: 1.06 us -> 0.03 us
where the time goes in v3:
time: 83 us; the launch traced here: 82.8 us
  blocking collectives  44.1 us (53%)
  starting transfers between devices  16.5 us (20%)
  Pallas kernels  11.7 us (14%)
  waiting for transfers between devices  8.81 us (11%)
  between operations  1.35 us (2%)
    all_to_all x3, blocking collectives, exchange(): lax.all_to_all(value, 'dp', 0, 0, axis_index_groups=groups, tiled=True)  44.1 us
    ppermute x3, starting transfers between devices, swap_cores(): return lax.ppermute(value, 'dp', [(i, i ^ 1) for i in range(64)])  9.44 us
    pallas_call x1, Pallas kernels, gram(): pl.pallas_call(gram_kernel, out_shape=(half, half), in_specs=[pl.BlockSpe...  7.44 us
    ppermute x2, starting transfers between devices, group_sum(): value = value + lax.ppermute(value, 'grp', [(i, i ^ k) for i in range(4)])  7.05 us
    ppermute x3, waiting for transfers between devices, swap_cores(): return lax.ppermute(value, 'dp', [(i, i ^ 1) for i in range(64)])  4.89 us
    ppermute x2, waiting for transfers between devices, group_sum(): value = value + lax.ppermute(value, 'grp', [(i, i ^ k) for i in range(4)])  3.92 us
    pallas_call x1, Pallas kernels, precondition(): pl.pallas_call(precond_kernel, out_shape=(jax.ShapeDtypeStruct((1, DG, DG...  2.51 us
  transfers between devices with their start and end apart: 5, of which 5 were waited for; matrix products, arithmetic and copies ran while one was open for 0% of the time, Pallas kernels for 1%

profile of v3, /device:TPU:1, one launch (start us, length us, event | category | flops | bytes accessed | tf_op | source)
XLA Modules:
  0.0 82.8 jit_solution(6881481588624785138)
XLA Ops:
  1.3 7.4 %gram.1 = (f32[4,8,14,8,128]{4,3,2,1,0:T(8,128)S(1)}, f32[4,8,14,8,128]{4,3,2,1,0:T(8,128)S(1)}) custom-call(s32[1]{0:T(128)S(6)} %copy.10.count_ref, bf16[1,2048,1152]{2,1,0:T(8,128)(2,1)} %x_hbm.1, bf16[1,2048,128]{2,1,0:T(8,128)(2,1)} %y_hbm.1), custom_call_target="tpu_custom_call" | custom-call | flops 6710886400 | bytes 10485760 | tf_op jit(solution)/shard_map/gram/pallas_call | solution.py:119
  8.7 3.3 %collective-permute-start = (f32[4,8,14,8,128]{4,3,2,1,0:T(8,128)S(1)}, f32[4,8,14,8,128]{4,3,2,1,0:T(8,128)S(1)}, u32[]{:S(2)}, u32[]{:S(2)}) collective-permute-start(f32[4,8,14,8,128]{4,3,2,1,0:T(8,128)S(1)} %get-tuple-element.11), channel_id=1, source_target_pairs={{0,4},{4,0},{8,12},{12,8},{16,20},{20,16},{24,28},{28,24},{32,36},... | collective-permute-start | bytes 5505032 | tf_op jit(solution)/shard_map/ppermute | solution.py:282
  12.1 3.4 %collective-permute-done = f32[4,8,14,8,128]{4,3,2,1,0:T(8,128)S(1)} collective-permute-done((f32[4,8,14,8,128]{4,3,2,1,0:T(8,128)S(1)}, f32[4,8,14,8,128]{4,3,2,1,0:T(8,128)S(1)}, u32[]{:S(2)}, u32[]{:S(2)}) %collective-permute-start) | collective-permute-done | bytes 1835040 | tf_op jit(solution)/shard_map/ppermute | solution.py:282
  15.5 0.3 add.9
  15.8 16.7 %all_to_all.15.met = f32[4,8,14,8,128]{4,3,2,1,0:T(8,128)S(1)} all-to-all(f32[4,8,14,8,128]{4,3,2,1,0:T(8,128)S(1)} %add.9), channel_id=1, replica_groups={{0,8,16,24},{32,40,48,56},{64,72,80,88},{96,104,112,120},{128,136,144,1..., dimensions={0} | all-to-all | bytes 3670016 | tf_op jit(solution)/shard_map/all_to_all | solution.py:292
  32.5 0.1 collect.2
  32.6 0.0 copy-start
  32.6 0.0 copy-start.1
  32.6 0.0 copy-start.2
  32.6 0.0 copy-start.3
  32.6 13.5 %all_to_all.16.met = f32[8,14,8,128]{3,2,1,0:T(8,128)S(1)} all-to-all(f32[8,14,8,128]{3,2,1,0:T(8,128)S(1)} %collect.2), channel_id=1, replica_groups={{0,32,64,96,128,160,192,224},{8,40,72,104,136,168,200,232},{16,48,80,11..., dimensions={0} | all-to-all | bytes 917504 | tf_op jit(solution)/shard_map/all_to_all | solution.py:292
  46.1 3.1 %collective-permute-start.1 = (f32[14,8,128]{2,1,0:T(8,128)S(1)}, f32[14,8,128]{2,1,0:T(8,128)S(1)}, u32[]{:S(2)}, u32[]{:S(2)}) collective-permute-start(f32[14,8,128]{2,1,0:T(8,128)S(1)} %collect.3), channel_id=1, source_target_pairs={{0,1},{1,0},{2,3},{3,2},{4,5},{5,4},{6,7},{7,6},{8,9},{9,8},{10,11... | collective-permute-start | bytes 172040 | tf_op jit(solution)/shard_map/ppermute | solution.py:287
  49.2 2.2 %collective-permute-done.1 = f32[14,8,128]{2,1,0:T(8,128)S(1)} collective-permute-done((f32[14,8,128]{2,1,0:T(8,128)S(1)}, f32[14,8,128]{2,1,0:T(8,128)S(1)}, u32[]{:S(2)}, u32[]{:S(2)}) %collective-permute-start.1) | collective-permute-done | bytes 57376 | tf_op jit(solution)/shard_map/ppermute | solution.py:287
  51.4 4.0 %collective-permute-start.2 = (f32[14,8,128]{2,1,0:T(8,128)S(1)}, f32[14,8,128]{2,1,0:T(8,128)S(1)}, u32[]{:S(2)}, u32[]{:S(2)}) collective-permute-start(f32[14,8,128]{2,1,0:T(8,128)S(1)} %add.10), channel_id=1, source_target_pairs={{0,3},{1,2},{2,1},{3,0},{4,7},{5,6},{6,5},{7,4},{8,11},{9,10},{10,... | collective-permute-start | bytes 172040 | tf_op jit(solution)/shard_map/ppermute | solution.py:287
  55.4 1.7 %collective-permute-done.2 = f32[14,8,128]{2,1,0:T(8,128)S(1)} collective-permute-done((f32[14,8,128]{2,1,0:T(8,128)S(1)}, f32[14,8,128]{2,1,0:T(8,128)S(1)}, u32[]{:S(2)}, u32[]{:S(2)}) %collective-permute-start.2) | collective-permute-done | bytes 57376 | tf_op jit(solution)/shard_map/ppermute | solution.py:287
  57.1 3.9 %collective-permute-start.3 = (f32[14,8,128]{2,1,0:T(8,128)S(1)}, f32[14,8,128]{2,1,0:T(8,128)S(1)}, u32[]{:S(2)}, u32[]{:S(2)}) collective-permute-start(f32[14,8,128]{2,1,0:T(8,128)S(1)} %add.11.done), channel_id=1, source_target_pairs={{0,4},{4,0},{8,12},{12,8},{16,20},{20,16},{24,28},{28,24},{32,36},... | collective-permute-start | bytes 172040 | tf_op jit(solution)/shard_map/ppermute | solution.py:282
  61.0 0.9 %collective-permute-done.3.twin = f32[14,8,128]{2,1,0:T(8,128)S(1)} collective-permute-done((f32[14,8,128]{2,1,0:T(8,128)S(1)}, f32[14,8,128]{2,1,0:T(8,128)S(1)}, u32[]{:S(2)}, u32[]{:S(2)}) %collective-permute-start.3) | collective-permute-done | bytes 57376 | tf_op jit(solution)/shard_map/ppermute | solution.py:282
  61.9 0.7 spread.1
  62.6 13.9 %all_to_all.17.got = f32[32,4,8,128]{3,2,1,0:T(8,128)S(1)} all-to-all(f32[32,4,8,128]{3,2,1,0:T(8,128)S(1)} %get-tuple-element.12), channel_id=1, replica_groups={{0,8,16,24,32,40,48,56,64,72,80,88,96,104,112,120,128,136,144,152,160,1..., dimensions={0} | all-to-all | bytes 1048576 | tf_op jit(solution)/shard_map/all_to_all | solution.py:292
  76.5 2.2 %collective-permute-start.4 = (f32[32,4,8,128]{3,2,1,0:T(8,128)S(1)}, f32[32,4,8,128]{3,2,1,0:T(8,128)S(1)}, u32[]{:S(2)}, u32[]{:S(2)}) collective-permute-start(f32[32,4,8,128]{3,2,1,0:T(8,128)S(1)} %all_to_all.17.got), channel_id=1, source_target_pairs={{0,4},{4,0},{8,12},{12,8},{16,20},{20,16},{24,28},{28,24},{32,36},... | collective-permute-start | bytes 1572872 | tf_op jit(solution)/shard_map/ppermute | solution.py:282
  78.7 0.9 %factor_rows.1 = f32[18,1,1152]{2,1,0:T(1,128)} custom-call(f32[32,4,8,128]{3,2,1,0:T(8,128)S(1)} %all_to_all.17.got, f32[9,40,128]{2,1,0:T(8,128)S(1)} %get-tuple-element.13.direct, f32[8,128]{1,0:T(8,128)S(1)} %get-tuple-element.14.total_ref), custom_call_target="tpu_custom_call" | custom-call | flops 1000000 | bytes 1048576 | tf_op jit(solution)/shard_map/factor_rows/pallas_call | solution.py:237
  79.7 0.6 collective-permute-done.4.other
  80.3 0.0 copy-done
  80.3 0.0 copy-done.1
  80.3 0.0 copy-done.2
  80.3 0.0 copy-done.3
  80.3 2.5 %precondition.1 = (f32[1,128,128]{2,1,0:T(8,128)}, f32[1,128,1152]{2,1,0:T(8,128)}) custom-call(f32[32,4,8,128]{3,2,1,0:T(8,128)S(1)} %all_to_all.17.got, f32[32,4,8,128]{3,2,1,0:T(8,128)S(1)} %collective-permute-done.4.other, f32[8,128]{1,0:T(8,128)S(1)} %get-tuple-element.14.total_ref, bf16[1,1152,1152]{2,1,0:T(8,128)(2,1)S(1)} %copy-done, ...), custom_call_target="tpu_custom_call" | custom-call | tf_op jit(solution)/shard_map/precondition/pallas_call | solution.py:272
  (3 shorter events, 0.0 us)
Async XLA Ops:
  8.7 6.7 %collective-permute-start = (f32[4,8,14,8,128]{4,3,2,1,0:T(8,128)S(1)}, f32[4,8,14,8,128]{4,3,2,1,0:T(8,128)S(1)}, u32[]{:S(2)}, u32[]{:S(2)}) collective-permute-start(f32[4,8,14,8,128]{4,3,2,1,0:T(8,128)S(1)} %get-tuple-element.11), channel_id=1, source_target_pairs={{0,4},{4,0},{8,12},{12,8},{16,20},{20,16},{24,28},{28,24},{32,36},... | collective-permute-start | bytes 5505032 | tf_op jit(solution)/shard_map/ppermute | solution.py:282
  32.6 47.7 %copy-start = (bf16[1,1152,1152]{2,1,0:T(8,128)(2,1)S(1)}, bf16[1,1152,1152]{2,1,0:T(8,128)(2,1)}, u32[]{:S(2)}) copy-start(bf16[1,1152,1152]{2,1,0:T(8,128)(2,1)} %basis_a.1) | copy-start | bytes 7962628
  32.6 47.7 %copy-start.1 = (bf16[1,128,128]{2,1,0:T(8,128)(2,1)S(1)}, bf16[1,128,128]{2,1,0:T(8,128)(2,1)}, u32[]{:S(2)}) copy-start(bf16[1,128,128]{2,1,0:T(8,128)(2,1)} %basis_g.1) | copy-start | bytes 98308
  32.6 47.7 %copy-start.2 = (f32[1,1152]{1,0:T(1,128)S(1)}, f32[1,1152]{1,0:T(1,128)}, u32[]{:S(2)}) copy-start(f32[1,1152]{1,0:T(1,128)} %eig_a.1) | copy-start | bytes 13828
  32.6 47.7 %copy-start.3 = (f32[1,128]{1,0:T(1,128)S(1)}, f32[1,128]{1,0:T(1,128)}, u32[]{:S(2)}) copy-start(f32[1,128]{1,0:T(1,128)} %eig_g.1) | copy-start | bytes 1540
  46.1 5.3 %collective-permute-start.1 = (f32[14,8,128]{2,1,0:T(8,128)S(1)}, f32[14,8,128]{2,1,0:T(8,128)S(1)}, u32[]{:S(2)}, u32[]{:S(2)}) collective-permute-start(f32[14,8,128]{2,1,0:T(8,128)S(1)} %collect.3), channel_id=1, source_target_pairs={{0,1},{1,0},{2,3},{3,2},{4,5},{5,4},{6,7},{7,6},{8,9},{9,8},{10,11... | collective-permute-start | bytes 172040 | tf_op jit(solution)/shard_map/ppermute | solution.py:287
  51.4 5.7 %collective-permute-start.2 = (f32[14,8,128]{2,1,0:T(8,128)S(1)}, f32[14,8,128]{2,1,0:T(8,128)S(1)}, u32[]{:S(2)}, u32[]{:S(2)}) collective-permute-start(f32[14,8,128]{2,1,0:T(8,128)S(1)} %add.10), channel_id=1, source_target_pairs={{0,3},{1,2},{2,1},{3,0},{4,7},{5,6},{6,5},{7,4},{8,11},{9,10},{10,... | collective-permute-start | bytes 172040 | tf_op jit(solution)/shard_map/ppermute | solution.py:287
  57.1 4.8 %collective-permute-start.3 = (f32[14,8,128]{2,1,0:T(8,128)S(1)}, f32[14,8,128]{2,1,0:T(8,128)S(1)}, u32[]{:S(2)}, u32[]{:S(2)}) collective-permute-start(f32[14,8,128]{2,1,0:T(8,128)S(1)} %add.11.done), channel_id=1, source_target_pairs={{0,4},{4,0},{8,12},{12,8},{16,20},{20,16},{24,28},{28,24},{32,36},... | collective-permute-start | bytes 172040 | tf_op jit(solution)/shard_map/ppermute | solution.py:282
  76.5 3.8 %collective-permute-start.4 = (f32[32,4,8,128]{3,2,1,0:T(8,128)S(1)}, f32[32,4,8,128]{3,2,1,0:T(8,128)S(1)}, u32[]{:S(2)}, u32[]{:S(2)}) collective-permute-start(f32[32,4,8,128]{3,2,1,0:T(8,128)S(1)} %all_to_all.17.got), channel_id=1, source_target_pairs={{0,4},{4,0},{8,12},{12,8},{16,20},{20,16},{24,28},{28,24},{32,36},... | collective-permute-start | bytes 1572872 | tf_op jit(solution)/shard_map/ppermute | solution.py:282

commit v4 on v3

--- a/solution.py
+++ b/solution.py
@@ -203,7 +203,8 @@
     )(done, twin)
 
 
-def rows_kernel(got, direct, total_ref, out, turned):
+def rows_kernel(got, direct, total_ref, eig_a, eig_g, out, scale, turned):
+    scale[...] = 1.0 / (jnp.broadcast_to(eig_g[...], (DG, DG)).T[:, 0:1] * eig_a[...] + 0.001)
     group, xl, core = position()
     total = total_ref[0:1, 0:1]
     for n in range(CHIPS):
@@ -232,23 +233,24 @@
                     out[i, :, lanes] = value[i : i + 1, :]
 
 
-def factor_rows(got, direct, total):
+def factor_rows(got, direct, total, eig_a, eig_g):
     vmem = pl.BlockSpec(memory_space=pltpu.VMEM)
-    out = pl.pallas_call(
+    out, scale = pl.pallas_call(
         rows_kernel,
-        out_shape=jax.ShapeDtypeStruct((18, 1, DA), F32),
-        in_specs=[vmem] * 3,
+        out_shape=(jax.ShapeDtypeStruct((18, 1, DA), F32), jax.ShapeDtypeStruct((DG, DA), F32)),
+        in_specs=[vmem] * 5,
+        out_specs=(vmem, vmem),
         scratch_shapes=[pltpu.VMEM((24, DA), F32)],
         compiler_params=pltpu.CompilerParams(vmem_limit_bytes=16 * 2**20),
         cost_estimate=pl.CostEstimate(flops=10**6, bytes_accessed=2**20, transcendentals=0),
         name="factor_rows",
-    )(got, direct, total)
-    return out.reshape(1, 18, DA)
-
-
-def precond_kernel(got, other, total_ref, basis_a, basis_g, eig_a, eig_g, g_factor, precond):
+    )(got, direct, total, eig_a, eig_g)
+    return out.reshape(1, 18, DA), scale
+
+
+def precond_kernel(got, other, total_ref, basis_a, basis_g, scale, g_factor, precond):
     core = lax.rem(lax.axis_index("dp"), 2)
-    total = total_ref[0:1, 0:1]
+    share = 1.0 / total_ref[0:1, 0:1]
     shape = (16, 2, GRADS + 1, 8, 128)
     both = (got[...].reshape(shape), other[...].reshape(shape))
     columns = []
@@ -256,26 +258,25 @@
         n, rest = divmod(col, 5)
         low, rest = (rest < 3), (rest if rest < 3 else rest - 3)
         tiles = jnp.where((core == 0) == low, both[0][:, n, rest], both[1][:, n, rest])
-        columns.append(tiles.reshape(128, 128) / total)
+        columns.append(tiles.reshape(128, 128) * share)
     g_factor[0] = columns[-1]
     grad = jnp.concatenate([c.astype(BF16) for c in columns[:-1]], axis=1)
     left = lax.dot_general(basis_g[0], grad, (((0,), (0,)), ((), ())), preferred_element_type=F32).astype(BF16)
     rotated = jnp.dot(left, basis_a[0], preferred_element_type=F32)
-    eig_rows = jnp.broadcast_to(eig_g[...], (DG, DG)).T[:, 0:1]
-    scaled = (rotated / (eig_rows * eig_a[...] + 0.001)).astype(BF16)
+    scaled = (rotated * scale[...]).astype(BF16)
     inner = jnp.dot(basis_g[0], scaled, preferred_element_type=F32).astype(BF16)
     precond[0] = lax.dot_general(inner, basis_a[0], (((1,), (1,)), ((), ())), preferred_element_type=F32)
 
 
-def precondition(got, other, total, basis_a, basis_g, eig_a, eig_g):
+def precondition(got, other, total, basis_a, basis_g, scale):
     vmem = pl.BlockSpec(memory_space=pltpu.VMEM)
     return pl.pallas_call(
         precond_kernel,
         out_shape=(jax.ShapeDtypeStruct((1, DG, DG), F32), jax.ShapeDtypeStruct((1, DG, DA), F32)),
-        in_specs=[vmem] * 7,
+        in_specs=[vmem] * 6,
         compiler_params=pltpu.CompilerParams(vmem_limit_bytes=16 * 2**20),
         name="precondition",
-    )(got, other, total, basis_a, basis_g, eig_a, eig_g)
+    )(got, other, total, basis_a, basis_g, scale)
 
 
 def swap_cores(value):
@@ -299,8 +300,8 @@
     send, direct, total = spread(done, swap_cores(done))
     got = exchange(send, CHIP_GROUPS)
     other = swap_cores(got)
-    a_factor = factor_rows(got, direct, total)
-    g_factor, precond = precondition(got, other, total, basis_a, basis_g, eig_a, eig_g)
+    a_factor, scale = factor_rows(got, direct, total, eig_a, eig_g)
+    g_factor, precond = precondition(got, other, total, basis_a, basis_g, scale)
     return a_factor, g_factor, precond
 
 

time: 83 us -> 83 us (level)
  no operation moved by 1% of the time
where the time goes in v4:
time: 83 us; the launch traced here: 82.8 us
  blocking collectives  44.1 us (53%)
  starting transfers between devices  16.5 us (20%)
  Pallas kernels  11.7 us (14%)
  waiting for transfers between devices  8.74 us (11%)
  between operations  1.34 us (2%)
    all_to_all x3, blocking collectives, exchange(): lax.all_to_all(value, 'dp', 0, 0, axis_index_groups=groups, tiled=True)  44.1 us
    ppermute x3, starting transfers between devices, swap_cores(): return lax.ppermute(value, 'dp', [(i, i ^ 1) for i in range(64)])  9.45 us
    pallas_call x1, Pallas kernels, gram(): pl.pallas_call(gram_kernel, out_shape=(half, half), in_specs=[pl.BlockSpe...  7.44 us
    ppermute x2, starting transfers between devices, group_sum(): value = value + lax.ppermute(value, 'grp', [(i, i ^ k) for i in range(4)])  7.05 us
    ppermute x3, waiting for transfers between devices, swap_cores(): return lax.ppermute(value, 'dp', [(i, i ^ 1) for i in range(64)])  4.82 us
    ppermute x2, waiting for transfers between devices, group_sum(): value = value + lax.ppermute(value, 'grp', [(i, i ^ k) for i in range(4)])  3.92 us
    pallas_call x1, Pallas kernels, precondition(): pl.pallas_call(precond_kernel, out_shape=(jax.ShapeDtypeStruct((1, DG, DG...  2.51 us
  transfers between devices with their start and end apart: 5, of which 5 were waited for; matrix products, arithmetic and copies ran while one was open for 0% of the time, Pallas kernels for 1%

profile of v4, /device:TPU:1, one launch (start us, length us, event | category | flops | bytes accessed | tf_op | source)
XLA Modules:
  0.0 82.8 jit_solution(13068889606698882018)
XLA Ops:
  1.3 7.4 %gram.1 = (f32[4,8,14,8,128]{4,3,2,1,0:T(8,128)S(1)}, f32[4,8,14,8,128]{4,3,2,1,0:T(8,128)S(1)}) custom-call(s32[1]{0:T(128)S(6)} %copy.10.count_ref, bf16[1,2048,1152]{2,1,0:T(8,128)(2,1)} %x_hbm.1, bf16[1,2048,128]{2,1,0:T(8,128)(2,1)} %y_hbm.1), custom_call_target="tpu_custom_call" | custom-call | flops 6710886400 | bytes 10485760 | tf_op jit(solution)/shard_map/gram/pallas_call | solution.py:119
  8.7 3.3 %collective-permute-start = (f32[4,8,14,8,128]{4,3,2,1,0:T(8,128)S(1)}, f32[4,8,14,8,128]{4,3,2,1,0:T(8,128)S(1)}, u32[]{:S(2)}, u32[]{:S(2)}) collective-permute-start(f32[4,8,14,8,128]{4,3,2,1,0:T(8,128)S(1)} %get-tuple-element.13), channel_id=1, source_target_pairs={{0,4},{4,0},{8,12},{12,8},{16,20},{20,16},{24,28},{28,24},{32,36},... | collective-permute-start | bytes 5505032 | tf_op jit(solution)/shard_map/ppermute | solution.py:283
  12.1 3.4 %collective-permute-done = f32[4,8,14,8,128]{4,3,2,1,0:T(8,128)S(1)} collective-permute-done((f32[4,8,14,8,128]{4,3,2,1,0:T(8,128)S(1)}, f32[4,8,14,8,128]{4,3,2,1,0:T(8,128)S(1)}, u32[]{:S(2)}, u32[]{:S(2)}) %collective-permute-start) | collective-permute-done | bytes 1835040 | tf_op jit(solution)/shard_map/ppermute | solution.py:283
  15.5 0.3 add.9
  15.8 16.7 %all_to_all.15.met = f32[4,8,14,8,128]{4,3,2,1,0:T(8,128)S(1)} all-to-all(f32[4,8,14,8,128]{4,3,2,1,0:T(8,128)S(1)} %add.9), channel_id=1, replica_groups={{0,8,16,24},{32,40,48,56},{64,72,80,88},{96,104,112,120},{128,136,144,1..., dimensions={0} | all-to-all | bytes 3670016 | tf_op jit(solution)/shard_map/all_to_all | solution.py:293
  32.5 0.1 collect.2
  32.6 0.0 copy-start.2
  32.6 0.0 copy-start.3
  32.6 0.0 copy-start
  32.6 0.0 copy-start.1
  32.6 13.5 %all_to_all.16.met = f32[8,14,8,128]{3,2,1,0:T(8,128)S(1)} all-to-all(f32[8,14,8,128]{3,2,1,0:T(8,128)S(1)} %collect.2), channel_id=1, replica_groups={{0,32,64,96,128,160,192,224},{8,40,72,104,136,168,200,232},{16,48,80,11..., dimensions={0} | all-to-all | bytes 917504 | tf_op jit(solution)/shard_map/all_to_all | solution.py:293
  46.1 3.1 %collective-permute-start.1 = (f32[14,8,128]{2,1,0:T(8,128)S(1)}, f32[14,8,128]{2,1,0:T(8,128)S(1)}, u32[]{:S(2)}, u32[]{:S(2)}) collective-permute-start(f32[14,8,128]{2,1,0:T(8,128)S(1)} %collect.3), channel_id=1, source_target_pairs={{0,1},{1,0},{2,3},{3,2},{4,5},{5,4},{6,7},{7,6},{8,9},{9,8},{10,11... | collective-permute-start | bytes 172040 | tf_op jit(solution)/shard_map/ppermute | solution.py:288
  49.2 2.2 %collective-permute-done.1 = f32[14,8,128]{2,1,0:T(8,128)S(1)} collective-permute-done((f32[14,8,128]{2,1,0:T(8,128)S(1)}, f32[14,8,128]{2,1,0:T(8,128)S(1)}, u32[]{:S(2)}, u32[]{:S(2)}) %collective-permute-start.1) | collective-permute-done | bytes 57376 | tf_op jit(solution)/shard_map/ppermute | solution.py:288
  51.4 4.0 %collective-permute-start.2 = (f32[14,8,128]{2,1,0:T(8,128)S(1)}, f32[14,8,128]{2,1,0:T(8,128)S(1)}, u32[]{:S(2)}, u32[]{:S(2)}) collective-permute-start(f32[14,8,128]{2,1,0:T(8,128)S(1)} %add.10), channel_id=1, source_target_pairs={{0,3},{1,2},{2,1},{3,0},{4,7},{5,6},{6,5},{7,4},{8,11},{9,10},{10,... | collective-permute-start | bytes 172040 | tf_op jit(solution)/shard_map/ppermute | solution.py:288
  55.4 1.7 %collective-permute-done.2 = f32[14,8,128]{2,1,0:T(8,128)S(1)} collective-permute-done((f32[14,8,128]{2,1,0:T(8,128)S(1)}, f32[14,8,128]{2,1,0:T(8,128)S(1)}, u32[]{:S(2)}, u32[]{:S(2)}) %collective-permute-start.2) | collective-permute-done | bytes 57376 | tf_op jit(solution)/shard_map/ppermute | solution.py:288
  57.1 3.9 %collective-permute-start.3 = (f32[14,8,128]{2,1,0:T(8,128)S(1)}, f32[14,8,128]{2,1,0:T(8,128)S(1)}, u32[]{:S(2)}, u32[]{:S(2)}) collective-permute-start(f32[14,8,128]{2,1,0:T(8,128)S(1)} %add.11.done), channel_id=1, source_target_pairs={{0,4},{4,0},{8,12},{12,8},{16,20},{20,16},{24,28},{28,24},{32,36},... | collective-permute-start | bytes 172040 | tf_op jit(solution)/shard_map/ppermute | solution.py:283
  61.0 0.9 %collective-permute-done.3.twin = f32[14,8,128]{2,1,0:T(8,128)S(1)} collective-permute-done((f32[14,8,128]{2,1,0:T(8,128)S(1)}, f32[14,8,128]{2,1,0:T(8,128)S(1)}, u32[]{:S(2)}, u32[]{:S(2)}) %collective-permute-start.3) | collective-permute-done | bytes 57376 | tf_op jit(solution)/shard_map/ppermute | solution.py:283
  61.9 0.7 spread.1
  62.6 13.9 %all_to_all.17.got = f32[32,4,8,128]{3,2,1,0:T(8,128)S(1)} all-to-all(f32[32,4,8,128]{3,2,1,0:T(8,128)S(1)} %get-tuple-element.14), channel_id=1, replica_groups={{0,8,16,24,32,40,48,56,64,72,80,88,96,104,112,120,128,136,144,152,160,1..., dimensions={0} | all-to-all | bytes 1048576 | tf_op jit(solution)/shard_map/all_to_all | solution.py:293
  76.5 2.2 %collective-permute-start.4 = (f32[32,4,8,128]{3,2,1,0:T(8,128)S(1)}, f32[32,4,8,128]{3,2,1,0:T(8,128)S(1)}, u32[]{:S(2)}, u32[]{:S(2)}) collective-permute-start(f32[32,4,8,128]{3,2,1,0:T(8,128)S(1)} %all_to_all.17.got), channel_id=1, source_target_pairs={{0,4},{4,0},{8,12},{12,8},{16,20},{20,16},{24,28},{28,24},{32,36},... | collective-permute-start | bytes 1572872 | tf_op jit(solution)/shard_map/ppermute | solution.py:283
  78.7 0.0 copy-done.2
  78.7 0.0 copy-done.3
  78.7 1.0 %factor_rows.1 = (f32[18,1,1152]{2,1,0:T(1,128)}, f32[128,1152]{1,0:T(8,128)S(1)}) custom-call(f32[32,4,8,128]{3,2,1,0:T(8,128)S(1)} %all_to_all.17.got, f32[9,40,128]{2,1,0:T(8,128)S(1)} %get-tuple-element.15.direct, f32[8,128]{1,0:T(8,128)S(1)} %get-tuple-element.16.total_ref, f32[1,1152]{1,0:T(1,128)S(1)} %copy-done.2, f32[1,128]{1,0:T(1,128)S(1)} %copy-done.3), custom_call_target="tpu_custom_call" | custom-call | flops 1000000 | bytes 1048576 | tf_op jit(solution)/shard_map/factor_rows/pallas_call | solution.py:238
  79.7 0.5 collective-permute-done.4.other
  80.3 0.0 copy-done
  80.3 0.0 copy-done.1
  80.3 2.5 %precondition.1 = (f32[1,128,128]{2,1,0:T(8,128)}, f32[1,128,1152]{2,1,0:T(8,128)}) custom-call(f32[32,4,8,128]{3,2,1,0:T(8,128)S(1)} %all_to_all.17.got, f32[32,4,8,128]{3,2,1,0:T(8,128)S(1)} %collective-permute-done.4.other, f32[8,128]{1,0:T(8,128)S(1)} %get-tuple-element.16.total_ref, bf16[1,1152,1152]{2,1,0:T(8,128)(2,1)S(1)} %copy-done, ...), custom_call_target="tpu_custom_call" | custom-call | tf_op jit(solution)/shard_map/precondition/pallas_call | solution.py:273
  (3 shorter events, 0.0 us)
Async XLA Ops:
  8.7 6.7 %collective-permute-start = (f32[4,8,14,8,128]{4,3,2,1,0:T(8,128)S(1)}, f32[4,8,14,8,128]{4,3,2,1,0:T(8,128)S(1)}, u32[]{:S(2)}, u32[]{:S(2)}) collective-permute-start(f32[4,8,14,8,128]{4,3,2,1,0:T(8,128)S(1)} %get-tuple-element.13), channel_id=1, source_target_pairs={{0,4},{4,0},{8,12},{12,8},{16,20},{20,16},{24,28},{28,24},{32,36},... | collective-permute-start | bytes 5505032 | tf_op jit(solution)/shard_map/ppermute | solution.py:283
  32.6 46.2 %copy-start.2 = (f32[1,1152]{1,0:T(1,128)S(1)}, f32[1,1152]{1,0:T(1,128)}, u32[]{:S(2)}) copy-start(f32[1,1152]{1,0:T(1,128)} %eig_a.1) | copy-start | bytes 13828
  32.6 46.2 %copy-start.3 = (f32[1,128]{1,0:T(1,128)S(1)}, f32[1,128]{1,0:T(1,128)}, u32[]{:S(2)}) copy-start(f32[1,128]{1,0:T(1,128)} %eig_g.1) | copy-start | bytes 1540
  32.6 47.7 %copy-start = (bf16[1,1152,1152]{2,1,0:T(8,128)(2,1)S(1)}, bf16[1,1152,1152]{2,1,0:T(8,128)(2,1)}, u32[]{:S(2)}) copy-start(bf16[1,1152,1152]{2,1,0:T(8,128)(2,1)} %basis_a.1) | copy-start | bytes 7962628
  32.6 47.7 %copy-start.1 = (bf16[1,128,128]{2,1,0:T(8,128)(2,1)S(1)}, bf16[1,128,128]{2,1,0:T(8,128)(2,1)}, u32[]{:S(2)}) copy-start(bf16[1,128,128]{2,1,0:T(8,128)(2,1)} %basis_g.1) | copy-start | bytes 98308
  46.1 5.3 %collective-permute-start.1 = (f32[14,8,128]{2,1,0:T(8,128)S(1)}, f32[14,8,128]{2,1,0:T(8,128)S(1)}, u32[]{:S(2)}, u32[]{:S(2)}) collective-permute-start(f32[14,8,128]{2,1,0:T(8,128)S(1)} %collect.3), channel_id=1, source_target_pairs={{0,1},{1,0},{2,3},{3,2},{4,5},{5,4},{6,7},{7,6},{8,9},{9,8},{10,11... | collective-permute-start | bytes 172040 | tf_op jit(solution)/shard_map/ppermute | solution.py:288
  51.4 5.7 %collective-permute-start.2 = (f32[14,8,128]{2,1,0:T(8,128)S(1)}, f32[14,8,128]{2,1,0:T(8,128)S(1)}, u32[]{:S(2)}, u32[]{:S(2)}) collective-permute-start(f32[14,8,128]{2,1,0:T(8,128)S(1)} %add.10), channel_id=1, source_target_pairs={{0,3},{1,2},{2,1},{3,0},{4,7},{5,6},{6,5},{7,4},{8,11},{9,10},{10,... | collective-permute-start | bytes 172040 | tf_op jit(solution)/shard_map/ppermute | solution.py:288
  57.1 4.8 %collective-permute-start.3 = (f32[14,8,128]{2,1,0:T(8,128)S(1)}, f32[14,8,128]{2,1,0:T(8,128)S(1)}, u32[]{:S(2)}, u32[]{:S(2)}) collective-permute-start(f32[14,8,128]{2,1,0:T(8,128)S(1)} %add.11.done), channel_id=1, source_target_pairs={{0,4},{4,0},{8,12},{12,8},{16,20},{20,16},{24,28},{28,24},{32,36},... | collective-permute-start | bytes 172040 | tf_op jit(solution)/shard_map/ppermute | solution.py:283
  76.5 3.8 %collective-permute-start.4 = (f32[32,4,8,128]{3,2,1,0:T(8,128)S(1)}, f32[32,4,8,128]{3,2,1,0:T(8,128)S(1)}, u32[]{:S(2)}, u32[]{:S(2)}) collective-permute-start(f32[32,4,8,128]{3,2,1,0:T(8,128)S(1)} %all_to_all.17.got), channel_id=1, source_target_pairs={{0,4},{4,0},{8,12},{12,8},{16,20},{20,16},{24,28},{28,24},{32,36},... | collective-permute-start | bytes 1572872 | tf_op jit(solution)/shard_map/ppermute | solution.py:283
